TPU v7x, 32 devices: a whole 2x2x4 slice. The times are simulated.
32 devices in a mesh: frame: 8 (over z, core), row: 4 (over y, x).
Axes of the slice: x: 2, y: 2, z: 4, core: 2. Of those that a mesh axis runs over, the one named last changes fastest.
Arguments:
- queries: bfloat16 [16, 16, 64, 2240], P('frame', 'row'), may hold values from -6 to 6
- keys: bfloat16 [16, 16, 64, 2240], P('frame', 'row'), may hold values from -12 to 12
- values: bfloat16 [16, 16, 64, 2240], P('frame', 'row'), may hold values from -12 to 12
- gate: bfloat16 [16, 16, 64, 2240], P('frame', 'row'), may hold values from -8 to 8
- conv_weight: float32 [3, 3, 2240], replicated, may hold values from -2 to 2
Outputs:
- mixed: bfloat16 [16, 16, 64, 2240], P('frame', 'row')
All inputs are finite; a program needn't handle non-finite values.
Results may differ from a plain program's by a relative error of at most 0.005.
Values may be sent and summed in bfloat16 or wider, within the bound.
No kernel may reach another device: no remote copies, remote signals or barrier semaphores. Data moves between devices by JAX's collectives and lax.ppermute only.
A program may use at most 128 MiB of HBM per device.

v0:
```python
import jax
import jax.numpy as jnp
from jax import lax
from jax.sharding import PartitionSpec as P

HEADS = 70
HEAD_DIM = 32


def prefix(array, axis, combine, identity):
    devices, position = (lax.axis_size(axis), lax.axis_index(axis))
    everything = jax.tree.map(lambda part: lax.all_gather(part, axis), array)
    start = jax.tree.map(
        lambda part, zero: jnp.broadcast_to(jnp.asarray(zero, part.dtype), part.shape),
        array,
        identity,
    )

    def step(k, before):
        reached = k < position
        new = combine(before, jax.tree.map(lambda part: part[k], everything))
        return jax.tree.map(lambda a, b: jnp.where(reached, a, b), new, before)

    return lax.fori_loop(0, devices, step, start)


def padded_2(array, sides, width):
    for axis, dim in sides:
        devices, length = (lax.axis_size(axis), array.shape[dim])
        up = [(i, (i + 1) % devices) for i in range(devices - 1)]
        down = [(j, i) for i, j in up]
        last = lax.slice_in_dim(array, length - width, length, axis=dim)
        leading = lax.slice_in_dim(array, 0, width, axis=dim)
        before = lax.ppermute(last, axis, up)
        after = lax.ppermute(leading, axis, down)
        array = jnp.concatenate([before, array, after], axis=dim)
    return array


def add_pair(earlier, later):
    return (earlier[0] + later[0], earlier[1] + later[1])


def per_device(queries, keys, values, gate, conv_weight):
    frames, rows, width, channels = queries.shape
    tokens = rows * width
    owner = jnp.arange(channels) // HEAD_DIM
    block = (owner[:, None] == owner[None, :]).astype(jnp.float32)
    head_sum = (owner[:, None] == jnp.arange(HEADS)[None, :]).astype(jnp.float32)
    kf = jax.nn.relu(keys).reshape(frames, tokens, channels)
    vf = values.reshape(frames, tokens, channels)

    def kv_state(pair):
        full = lax.dot_general(
            pair[0], pair[1], (((0,), (0,)), ((), ())), preferred_element_type=jnp.float32
        )
        return jnp.sum((full * block).reshape(HEADS, HEAD_DIM, channels), axis=0)

    partial_value = lax.map(kv_state, (kf, vf))
    norm_part = jnp.sum(kf, axis=1, dtype=jnp.float32)[:, None, :]
    partial_value, norm_part = (
        lax.psum_scatter(partial_value, "row", scatter_dimension=2, tiled=True),
        lax.psum_scatter(norm_part, "row", scatter_dimension=2, tiled=True),
    )
    totals = (jnp.sum(partial_value, axis=0), jnp.sum(norm_part, axis=0))
    identity = (jnp.zeros_like(totals[0]), jnp.zeros_like(totals[1]))
    before = prefix(totals, "frame", add_pair, identity)
    states = before[0][None] + jnp.cumsum(partial_value, axis=0)
    zsum = before[1][None] + jnp.cumsum(norm_part, axis=0)
    states, zsum = (
        lax.all_gather(states, "row", axis=2, tiled=True),
        lax.all_gather(zsum, "row", axis=2, tiled=True),
    )

    def read_frame(items):
        query, state, zrow = items
        qf = jax.nn.relu(query).astype(jnp.float32).reshape(tokens, channels)
        blocked = jnp.tile(state, (HEADS, 1)) * block
        numer = jnp.dot(qf, blocked, precision=lax.Precision.HIGHEST)
        per_head = jnp.dot(qf * zrow, head_sum, precision=lax.Precision.HIGHEST)
        denom = jnp.dot(per_head, head_sum.T, precision=lax.Precision.HIGHEST)
        return (numer / (denom + 1e-06)).reshape(rows, width, channels).astype(jnp.bfloat16)

    attended = lax.map(read_frame, (queries, states, zsum))
    padded = padded_2(attended, (("row", 1),), 1)
    mixes = []
    for b in range(3):
        total = jnp.zeros((frames, rows, width, channels), jnp.float32)
        for a in range(3):
            total = total + conv_weight[a, b] * padded[:, a : a + rows].astype(jnp.float32)
        mixes.append(total)
    column = jnp.zeros((frames, rows, 1, channels), jnp.float32)
    conv = mixes[1] + jnp.concatenate([column, mixes[0][:, :, :-1]], axis=2)
    conv = conv + jnp.concatenate([mixes[2][:, :, 1:], column], axis=2)
    return (conv * jax.nn.silu(gate.astype(jnp.float32))).astype(jnp.bfloat16)


def solution(mesh):
    in_specs = (
        P("frame", "row", None, None),
        P("frame", "row", None, None),
        P("frame", "row", None, None),
        P("frame", "row", None, None),
        P(),
    )
    out_specs = P("frame", "row", None, None)
    return jax.shard_map(
        per_device, mesh=mesh, in_specs=in_specs, out_specs=out_specs, check_vma=False
    )
```

profile of v0, /device:TPU:0, one launch (start us, length us, event | category | flops | bytes accessed | tf_op | source)
XLA Modules:
  0.0 307.5 jit_solution(6868422963782413608)
XLA Ops:
  6.5 0.0 all-reduce.7.cloned.1.call-start
  6.5 1.8 broadcast_maximum_fusion
  8.4 35.7 %while.46 = (s32[]{:T(128)}, f32[2,32,2240]{2,1,0:T(8,128)S(1)}, bf16[2,256,2240]{2,1,0:T(8,128)(2,1)S(1)}, bf16[2,256,2240]{2,1,0:T(8,128)(2,1)}, s32[2240]{0:T(1024)S(1)}) while((s32[]{:T(128)}, f32[2,32,2240]{2,1,0:T(8,128)S(1)}, bf16[2,256,2240]{2,1,0:T(8,128)(2,1)S(1)}, bf16[2,256,2240]{2,1,0:T(8,128)(2,1)}, ...), condition=%wide.region_2.3_spmd.clone.clone, body=%wide.region_0.2_spmd.clone.sunk.clone | while | flops 2583992320 | bytes 43402308 | solution.py:59
  8.4 9.9 %convolution_select_fusion.3 = f32[2240,2240]{1,0:T(8,128)} fusion(s32[2240]{0:T(1024)S(1)} %get-tuple-element.496, bf16[2,256,2240]{2,1,0:T(8,128)(2,1)} %get-tuple-element.495, s32[]{:T(128)} %get-tuple-element.487, bf16[2,256,2240]{2,1,0:T(8,128)(2,1)S(1)} %get-tuple-element.494), kind=kOutput, calls=%fused_computation.3.clone.1.clone | convolution fusion | flops 2579046400 | bytes 22455296 | tf_op jit(solution)/shard_map/while/body/eval_jaxpr/dot_general | solution.py:54
  18.3 7.8 %reduce_sum.45 = f32[32,2240]{1,0:T(8,128)S(1)} reduce(f32[70,32,2240]{2,1,0:T(8,128)} %bitcast.73, f32[]{:T(128)} %constant.90.clone.1..sunk.1), dimensions={0}, to_apply=%region_1.1 | reduce | flops 4945920 | bytes 20357124 | tf_op jit(solution)/shard_map/while/body/eval_jaxpr/reduce_sum | solution.py:57
  26.2 9.9 %convolution_select_fusion.3 = f32[2240,2240]{1,0:T(8,128)} fusion(s32[2240]{0:T(1024)S(1)} %get-tuple-element.496, bf16[2,256,2240]{2,1,0:T(8,128)(2,1)} %get-tuple-element.495, s32[]{:T(128)} %get-tuple-element.487, bf16[2,256,2240]{2,1,0:T(8,128)(2,1)S(1)} %get-tuple-element.494), kind=kOutput, calls=%fused_computation.3.clone.1.clone | convolution fusion | flops 2579046400 | bytes 22455296 | tf_op jit(solution)/shard_map/while/body/eval_jaxpr/dot_general | solution.py:54
  36.1 7.8 %reduce_sum.45 = f32[32,2240]{1,0:T(8,128)S(1)} reduce(f32[70,32,2240]{2,1,0:T(8,128)} %bitcast.73, f32[]{:T(128)} %constant.90.clone.1..sunk.1), dimensions={0}, to_apply=%region_1.1 | reduce | flops 4945920 | bytes 20357124 | tf_op jit(solution)/shard_map/while/body/eval_jaxpr/reduce_sum | solution.py:57
  44.0 0.0 copy-start.3
  44.0 0.0 copy-start.6
  44.1 0.0 copy-start.5
  44.1 0.8 copy-done.3
  44.8 0.0 all-reduce.7.cloned.1.call-update
  44.9 2.2 convert_reduce_fusion
  47.1 0.0 copy-done.6
  47.1 0.6 dynamic-slice.1
  48.5 0.0 copy-done.5
  48.5 0.6 dynamic-slice
  49.8 18.1 %all-reduce.4 = f32[2,1,2240]{2,1,0:T(1,128)S(1)} all-reduce(f32[2,1,2240]{2,1,0:T(1,128)S(1)} %broadcast_in_dim.32), channel_id=5, replica_groups=mesh['frame'=8,'row'=4] {'row'}, use_global_device_ids=true, to_apply=%region_6.7.clone | all-reduce | flops 4480 | bytes 35840
  67.9 0.1 dynamic-slice_reduce_fusion.2
  68.0 0.3 dynamic-update-slice
  68.3 25.9 %all-reduce.2 = f32[4480]{0:T(1024)S(1)} all-reduce(f32[4480]{0:T(1024)S(1)} %dynamic-update-slice), channel_id=3, replica_groups=mesh['frame'=8,'row'=4] {'frame'}, use_global_device_ids=true, to_apply=%add.2 | all-reduce | flops 4480 | bytes 35840
  94.2 0.1 reshape.128
  94.3 0.0 all-reduce.7.cloned.1.call-done
  94.4 1.0 dynamic-slice_reduce_fusion.1
  95.4 15.0 %all-gather = f32[256,560]{1,0:T(8,128)S(1)} all-gather(f32[32,560]{1,0:T(8,128)S(1)} %dynamic-slice_reduce_fusion.1), channel_id=2, replica_groups=mesh['frame'=8,'row'=4] {'frame'}, dimensions={0}, use_global_device_ids=true | all-gather | bytes 645120 | tf_op jit(solution)/shard_map/all_gather | solution.py:12
  110.4 0.5 while.47
  111.0 1.0 reduce-window_add_fusion
  112.0 0.2 copy.15
  112.3 24.5 %all_gather.22 = f32[2,32,2240]{1,0,2:T(2,128)S(1)} all-gather(f32[2,32,560]{1,0,2:T(2,128)S(1)} %copy.15), channel_id=1, replica_groups=mesh['frame'=8,'row'=4] {'row'}, dimensions={2}, use_global_device_ids=true | all-gather | bytes 716800 | tf_op jit(solution)/shard_map/all_gather | solution.py:71
  136.7 2.0 copy.17
  138.8 0.1 reduce-window_add_fusion.1
  138.9 0.2 copy.16
  139.0 12.7 %all_gather.23 = f32[2,1,2240]{0,1,2:T(1,128)S(1)} all-gather(f32[2,1,560]{0,1,2:T(1,128)S(1)} %copy.16), channel_id=1, replica_groups=mesh['frame'=8,'row'=4] {'row'}, dimensions={2}, use_global_device_ids=true | all-gather | bytes 22400 | tf_op jit(solution)/shard_map/all_gather | solution.py:72
  151.8 1.1 copy.18
  152.9 0.0 copy-start.4
  152.9 105.9 %while.48 = (s32[]{:T(128)}, bf16[2,4,64,2240]{3,2,1,0:T(8,128)(2,1)}, bf16[2,4,64,2240]{3,2,1,0:T(8,128)(2,1)}, f32[2,32,2240]{2,1,0:T(8,128)S(1)}, f32[2,1,2240]{2,1,0:T(1,128)S(1)}, /*index=5*/s32[2240]{0:T(1024)S(1)}) while((s32[]{:T(128)}, bf16[2,4,64,2240]{3,2,1,0:T(8,128)(2,1)}, ...), condition=%wide.region_13.14_spmd.clone.clone.clone.clone, body=%wide.region_12.13_spmd.clone.clone.clone.sunk.clone | while | flops 16396566528 | bytes 96281672 | solution.py:84
  153.0 8.3 %compare_convert_fusion.3 = f32[2240,2240]{1,0:T(8,128)} fusion(s32[2240]{0:T(1024)S(1)} %get-tuple-element.532), kind=kLoop, calls=%fused_computation.13.clone.1.clone | loop fusion | flops 10035200 | bytes 20079360 | tf_op jit(solution)/shard_map/convert_element_type | solution.py:48
  161.3 15.7 %broadcast_multiply_fusion.3 = f32[70,32,2240]{2,1,0:T(8,128)} fusion(f32[70,32,2240]{2,1,0:T(8,128)} %bitcast.75, f32[32,2240]{1,0:T(8,128)S(1)} %dynamic-slice_bitcast_fusion.3), kind=kLoop, calls=%fused_computation.14.clone.1.clone | loop fusion | flops 5017600 | bytes 40427520 | tf_op jit(solution)/shard_map/while/body/eval_jaxpr/mul | solution.py:78
  176.9 1.3 dynamic-slice_maximum_fusion.3
  178.3 20.4 %fusion.74 = f32[256,2240]{0,1:T(8,128)S(1)} fusion(bf16[256,2240]{1,0:T(8,128)(2,1)S(1)} %bitcast.76, f32[2240,2240]{1,0:T(8,128)} %bitcast.74), kind=kOutput, calls=%fused_computation.79.clone.1.clone | convolution fusion | flops 15414067200 | bytes 23511040 | tf_op jit(solution)/shard_map/while/body/eval_jaxpr/dot_general | solution.py:79
  198.7 2.7 fusion.75
  201.4 2.6 fusion.76
  204.0 0.7 copy.25
  204.8 1.2 constant_dynamic-update-slice_fusion.3
  206.0 8.3 %compare_convert_fusion.3 = f32[2240,2240]{1,0:T(8,128)} fusion(s32[2240]{0:T(1024)S(1)} %get-tuple-element.532), kind=kLoop, calls=%fused_computation.13.clone.1.clone | loop fusion | flops 10035200 | bytes 20079360 | tf_op jit(solution)/shard_map/convert_element_type | solution.py:48
  214.2 15.7 %broadcast_multiply_fusion.3 = f32[70,32,2240]{2,1,0:T(8,128)} fusion(f32[70,32,2240]{2,1,0:T(8,128)} %bitcast.75, f32[32,2240]{1,0:T(8,128)S(1)} %dynamic-slice_bitcast_fusion.3), kind=kLoop, calls=%fused_computation.14.clone.1.clone | loop fusion | flops 5017600 | bytes 40427520 | tf_op jit(solution)/shard_map/while/body/eval_jaxpr/mul | solution.py:78
  229.9 1.3 dynamic-slice_maximum_fusion.3
  231.2 20.4 %fusion.74 = f32[256,2240]{0,1:T(8,128)S(1)} fusion(bf16[256,2240]{1,0:T(8,128)(2,1)S(1)} %bitcast.76, f32[2240,2240]{1,0:T(8,128)} %bitcast.74), kind=kOutput, calls=%fused_computation.79.clone.1.clone | convolution fusion | flops 15414067200 | bytes 23511040 | tf_op jit(solution)/shard_map/while/body/eval_jaxpr/dot_general | solution.py:79
  251.7 2.7 fusion.75
  254.4 2.6 fusion.76
  257.0 0.7 copy.25
  257.7 1.1 constant_dynamic-update-slice_fusion.3
  258.8 1.5 fusion.39
  260.3 3.2 %collective-permute-start = (bf16[2,1,64,2240]{3,2,1,0:T(8,128)(2,1)S(1)}, bf16[2,1,64,2240]{3,2,1,0:T(8,128)(2,1)S(1)}, u32[]{:S(2)}, u32[]{:S(2)}) collective-permute-start(bf16[2,1,64,2240]{3,2,1,0:T(8,128)(2,1)S(1)} %get-tuple-element.333), channel_id=1, source_target_pairs={{0,1},{1,2},{2,3},{4,5},{5,6},{6,7},{8,9},{9,10},{10,11},{12,13},{... | collective-permute-start | bytes 1720328 | tf_op jit(solution)/shard_map/ppermute | solution.py:34
  263.5 1.5 collective-permute-start.1
  265.0 0.0 copy-done.4
  265.0 0.2 slice_reduce_fusion.8
  265.2 7.3 %collective-permute-done = bf16[2,1,64,2240]{3,2,1,0:T(8,128)(2,1)S(1)} collective-permute-done((bf16[2,1,64,2240]{3,2,1,0:T(8,128)(2,1)S(1)}, bf16[2,1,64,2240]{3,2,1,0:T(8,128)(2,1)S(1)}, u32[]{:S(2)}, u32[]{:S(2)}) %collective-permute-start) | collective-permute-done | bytes 573472 | tf_op jit(solution)/shard_map/ppermute | solution.py:34
  272.5 14.5 %collective-permute-done.1 = bf16[2,1,64,2240]{3,2,1,0:T(8,128)(2,1)S(1)} collective-permute-done((bf16[2,1,64,2240]{3,2,1,0:T(8,128)(2,1)S(1)}, bf16[2,1,64,2240]{3,2,1,0:T(8,128)(2,1)S(1)}, u32[]{:S(2)}, u32[]{:S(2)}) %collective-permute-start.1) | collective-permute-done | bytes 573472 | tf_op jit(solution)/shard_map/ppermute | solution.py:35
  286.9 1.4 fusion.31
  288.4 0.0 copy-done.1
  288.4 0.0 copy-done.2
  288.4 3.9 %fusion.27 = (f32[2,4,63,2240]{3,2,1,0:T(8,128)S(1)}, f32[2,4,63,2240]{3,2,1,0:T(8,128)}) fusion(f32[2,4,64,2240]{3,2,1,0:T(8,128)S(1)} %get-tuple-element.331, f32[2,4,64,2240]{3,2,1,0:T(8,128)S(1)} %get-tuple-element.332, f32[2,4,64,2240]{3,2,1,0:T(8,128)S(1)} %get-tuple-element.330, f32[2240]{0:T(1024)S(1)} %get-tuple-element.287, ...), kind=kLoop, calls=%fused_computation.43 | loop fusion | flops 11289600 | bytes 36180480 | tf_op jit(solution)/shard_map/add | solution.py:90
  292.3 8.4 %fusion.29 = bf16[2,4,64,2240]{3,2,1,0:T(8,128)(2,1)} fusion(bf16[2,4,64,2240]{3,2,1,0:T(8,128)(2,1)} %param.14, f32[2,4,63,2240]{3,2,1,0:T(8,128)} %get-tuple-element.329, f32[2,4,63,2240]{3,2,1,0:T(8,128)S(1)} %get-tuple-element.328, f32[2240]{0:T(1024)S(1)} %get-tuple-element.290, f32[2240]{0:T(1024)S(1)} %get-tuple-element.291, ...), kind=kLoop, calls=%fused_computation.48 | loop fusion | flops 21790720 | bytes 17086720 | tf_op jit(solution)/shard_map/convert_element_type | solution.py:95
  (34 shorter events, 0.5 us)
Async XLA Ops:
  6.5 87.8 %all-reduce.7.cloned.1.call-start = ((), (), s32[]{:S(2)}) async-start(), calls=%async_computation | async-start | bytes 1179648
  44.0 0.8 copy-start.3
  44.0 3.1 %copy-start.6 = (u32[32]{0:T(128)S(1)}, u32[32]{0:T(128)}, u32[]{:S(2)}) copy-start(u32[32]{0:T(128)} %constant.115) | copy-start | bytes 388
  44.1 4.4 %copy-start.5 = (u32[32]{0:T(128)S(1)}, u32[32]{0:T(128)}, u32[]{:S(2)}) copy-start(u32[32]{0:T(128)} %constant.108) | copy-start | bytes 388
  152.9 112.1 %copy-start.4 = (f32[3,3,2240]{2,1,0:T(4,128)S(1)}, f32[3,3,2240]{2,1,0:T(4,128)}, u32[]{:S(2)}) copy-start(f32[3,3,2240]{2,1,0:T(4,128)} %param.15) | copy-start | bytes 241924
  258.8 28.1 %copy-start = (bf16[2,4,64,2240]{3,2,1,0:T(8,128)(2,1)S(1)}, bf16[2,4,64,2240]{3,2,1,0:T(8,128)(2,1)}, u32[]{:S(2)}) copy-start(bf16[2,4,64,2240]{3,2,1,0:T(8,128)(2,1)} %get-tuple-element.185) | copy-start | bytes 6881284
  260.3 12.2 %collective-permute-start = (bf16[2,1,64,2240]{3,2,1,0:T(8,128)(2,1)S(1)}, bf16[2,1,64,2240]{3,2,1,0:T(8,128)(2,1)S(1)}, u32[]{:S(2)}, u32[]{:S(2)}) collective-permute-start(bf16[2,1,64,2240]{3,2,1,0:T(8,128)(2,1)S(1)} %get-tuple-element.333), channel_id=1, source_target_pairs={{0,1},{1,2},{2,3},{4,5},{5,6},{6,7},{8,9},{9,10},{10,11},{12,13},{... | collective-permute-start | bytes 1720328 | tf_op jit(solution)/shard_map/ppermute | solution.py:34
  263.5 23.5 %collective-permute-start.1 = (bf16[2,1,64,2240]{3,2,1,0:T(8,128)(2,1)S(1)}, bf16[2,1,64,2240]{3,2,1,0:T(8,128)(2,1)S(1)}, u32[]{:S(2)}, u32[]{:S(2)}) collective-permute-start(bf16[2,1,64,2240]{3,2,1,0:T(8,128)(2,1)S(1)} %get-tuple-element.334), channel_id=1, source_target_pairs={{1,0},{2,1},{3,2},{5,4},{6,5},{7,6},{9,8},{10,9},{11,10},{13,12},{... | collective-permute-start | bytes 1720328 | tf_op jit(solution)/shard_map/ppermute | solution.py:35
  272.5 15.9 %copy-start.1 = (bf16[2,1,64,2240]{3,2,1,0:T(8,128)(2,1)}, bf16[2,1,64,2240]{3,2,1,0:T(8,128)(2,1)S(1)}, u32[]{:S(2)}) copy-start(bf16[2,1,64,2240]{3,2,1,0:T(8,128)(2,1)S(1)} %collective-permute-done) | copy-start | bytes 1720324
  286.9 1.4 copy-start.2
Sparse Core Ops, SparseCore 0:
  45.0 49.1 all-reduce.6
where the time goes:
time: 308 us
  blocking collectives  96.2 us (31%)
  other arithmetic  86.6 us (28%)
  matrix products  71.2 us (23%)
  waiting for transfers between devices  21.8 us (7%)
  between operations  15 us (5%)
  local copies, waits for them, and re-layouts  11.7 us (4%)
  starting transfers between devices  4.67 us (2%)
    unnamed x2, blocking collectives  44 us
    dot_general x2, matrix products, read_frame(): numer = jnp.dot(qf, blocked, precision=lax.Precision.HIGHEST)  40.7 us
    mul x2, other arithmetic, read_frame(): blocked = jnp.tile(state, (HEADS, 1)) * block  31.3 us
    all_gather x1, blocking collectives, per_device(): lax.all_gather(states, 'row', axis=2, tiled=True)  24.5 us
    dot_general x2, matrix products, kv_state(): lax.dot_general(pair[0], pair[1], (((0,), (0,)), ((), ())), preferred_ele...  19.9 us
    convert_element_type x2, other arithmetic, per_device(): block = (owner[:, None] == owner[None, :]).astype(jnp.float32)  16.6 us
    reduce_sum x2, other arithmetic, kv_state(): return jnp.sum((full * block).reshape(HEADS, HEAD_DIM, channels), axis=0)  15.7 us
    all_gather x1, blocking collectives, prefix(): everything = jax.tree.map(lambda part: lax.all_gather(part, axis), array)  15 us
  transfers between devices with their start and end apart: 3, of which 2 were waited for; matrix products, arithmetic and copies ran while one was open for 1% of the time, Pallas kernels for 0%

commit v1 on v0

v1 whole, which is shorter than its diff:
```python
import functools

import jax
import jax.numpy as jnp
from jax import lax
from jax.experimental import pallas as pl
from jax.experimental.pallas import tpu as pltpu
from jax.sharding import PartitionSpec as P

HEAD_DIM = 32
LANES = 128
GROUP = LANES // HEAD_DIM
Z_ALIGN = 16


def ceil_div(a, b):
    return -(-a // b)


class Plan:
    def __init__(self, channels, halves):
        total = ceil_div(channels, LANES)
        self.channels = channels
        self.halves = halves
        self.blocks = ceil_div(total, halves)
        self.per = max(p for p in (1, 2, 3) if self.blocks % p == 0)
        self.steps = self.blocks // self.per
        self.z_row = self.blocks * HEAD_DIM
        self.rows = self.z_row + ceil_div(self.blocks, Z_ALIGN) * Z_ALIGN
        self.width = self.per * LANES


def same_head():
    row = lax.broadcasted_iota(jnp.int32, (LANES, LANES), 0) // HEAD_DIM
    col = lax.broadcasted_iota(jnp.int32, (LANES, LANES), 1) // HEAD_DIM
    return row == col


def sums_kernel(plan, frames, half_ref, k_ref, v_ref, o_ref, acc_ref):
    step = pl.program_id(0)
    mask = same_head()

    @pl.when(step == 0)
    def _():
        acc_ref[:, plan.z_row :, :] = jnp.zeros(
            (frames, plan.rows - plan.z_row, LANES), jnp.float32
        )

    for f in range(frames):
        for b in range(plan.per):
            lanes = slice(b * LANES, (b + 1) * LANES)
            kf = jnp.maximum(k_ref[f, :, lanes], 0)
            full = lax.dot_general(
                kf,
                v_ref[f, :, lanes],
                (((0,), (0,)), ((), ())),
                preferred_element_type=jnp.float32,
            )
            full = jnp.where(mask, full, 0.0)
            state = full.reshape(GROUP, HEAD_DIM, LANES).sum(axis=0)
            norm = jnp.sum(kf.astype(jnp.float32), axis=0, keepdims=True)
            block = step * plan.per + b
            acc_ref[f, pl.ds(pl.multiple_of(block * HEAD_DIM, HEAD_DIM), HEAD_DIM), :] = state
            acc_ref[f, pl.ds(plan.z_row + block, 1), :] = norm

    @pl.when(step == plan.steps - 1)
    def _():
        o_ref[...] = acc_ref[...].astype(o_ref.dtype)


def sums(plan, half, keys, values, dtype):
    frames, tokens, _ = keys.shape
    block = pl.BlockSpec(
        (frames, tokens, plan.width), lambda i, half: (0, 0, half[0] * plan.steps + i)
    )
    return pl.pallas_call(
        functools.partial(sums_kernel, plan, frames),
        grid_spec=pltpu.PrefetchScalarGridSpec(
            num_scalar_prefetch=1,
            grid=(plan.steps,),
            in_specs=[block, block],
            out_specs=pl.BlockSpec(
                (frames, plan.rows, LANES), lambda i, half: (0, 0, 0)
            ),
            scratch_shapes=[pltpu.VMEM((frames, plan.rows, LANES), jnp.float32)],
        ),
        out_shape=jax.ShapeDtypeStruct((frames, plan.rows, LANES), dtype),
        compiler_params=pltpu.CompilerParams(
            dimension_semantics=("arbitrary",), vmem_limit_bytes=32 << 20
        ),
        cost_estimate=pl.CostEstimate(
            flops=2 * frames * tokens * plan.blocks * LANES * LANES,
            bytes_accessed=4 * frames * tokens * plan.blocks * LANES,
            transcendentals=0,
        ),
        name="sums",
    )(half, keys, values)


def mix_kernel(plan, shape, half_ref, s_ref, q_ref, up_ref, down_ref, g_ref, w_ref, *rest):
    o_ref = rest[-1]
    frames, rows, width = shape
    step = pl.program_id(0)
    mask = same_head()
    ones = mask.astype(jnp.bfloat16)
    eye = lax.broadcasted_iota(jnp.int32, (LANES, LANES), 0) == lax.broadcasted_iota(
        jnp.int32, (LANES, LANES), 1
    )
    z_rows = plan.rows - plan.z_row
    z_iota = lax.broadcasted_iota(jnp.int32, (z_rows, LANES), 0)
    lane = lax.broadcasted_iota(jnp.int32, (1, LANES), 1)
    col = lax.broadcasted_iota(jnp.int32, (rows, width, LANES), 1)
    first = (half_ref[0] * plan.steps + step) * plan.width
    for f in range(frames):
        zs = s_ref[f, plan.z_row :, :].astype(jnp.float32)
        for b in range(plan.per):
            lanes = slice(b * LANES, (b + 1) * LANES)
            block = step * plan.per + b
            live = lane + (first + b * LANES) < plan.channels
            state = s_ref[f, pl.ds(pl.multiple_of(block * HEAD_DIM, HEAD_DIM), HEAD_DIM), :]
            tiled = jnp.concatenate([state.astype(jnp.float32)] * GROUP, axis=0)
            numer_w = jnp.where(mask & live, tiled, 0.0).astype(jnp.bfloat16)
            z = jnp.sum(jnp.where(z_iota == block, zs, 0.0), axis=0, keepdims=True)
            z = jnp.where(live, z, 0.0)
            diag = jnp.where(eye, z, 0.0).astype(jnp.bfloat16)
            denom_w = jnp.dot(diag, ones, preferred_element_type=jnp.float32).astype(jnp.bfloat16)
            weights = jnp.concatenate([numer_w, denom_w], axis=1)
            q = jnp.concatenate(
                [
                    up_ref[f, :, :, lanes].reshape(width, LANES),
                    q_ref[f, :, :, lanes].reshape(rows * width, LANES),
                    down_ref[f, :, :, lanes].reshape(width, LANES),
                ],
                axis=0,
            )
            qf = jnp.where(live, jnp.maximum(q, 0), jnp.zeros_like(q))
            both = jnp.dot(qf, weights, preferred_element_type=jnp.float32)
            att = both[:, :LANES] / (both[:, LANES:] + 1e-6)
            att = att.astype(jnp.bfloat16).astype(jnp.float32)
            att = att.reshape(rows + 2, width, LANES)
            mixes = []
            for c in range(3):
                total = att[0:rows] * w_ref[c, lanes]
                for a in range(1, 3):
                    total = total + att[a : a + rows] * w_ref[3 * a + c, lanes]
                mixes.append(total)
            conv = mixes[1]
            conv = conv + jnp.where(col == 0, 0.0, pltpu.roll(mixes[0], 1, axis=1))
            conv = conv + jnp.where(
                col == width - 1, 0.0, pltpu.roll(mixes[2], width - 1, axis=1)
            )
            g = g_ref[f, :, :, lanes].astype(jnp.float32)
            o_ref[f, :, :, lanes] = (conv * g / (1.0 + jnp.exp(-g))).astype(o_ref.dtype)


def mix(plan, half, states, queries, up, down, gate, weight, earlier):
    frames, rows, width, channels = queries.shape
    col = lambda i, half: (0, 0, 0, half[0] * plan.steps + i)
    body = pl.BlockSpec((frames, rows, width, plan.width), col)
    edge = pl.BlockSpec((frames, 1, width, plan.width), col)
    in_specs = [
        pl.BlockSpec((frames, plan.rows, LANES), lambda i, half: (0, 0, 0)),
        body,
        edge,
        edge,
        body,
        pl.BlockSpec((9, plan.width), lambda i, half: (0, half[0] * plan.steps + i)),
    ]
    operands = [states, queries, up, down, gate, weight]
    aliases = {}
    if earlier is not None:
        in_specs.append(pl.BlockSpec(memory_space=pl.ANY))
        operands.append(earlier)
        aliases = {7: 0}
    tokens = frames * (rows + 2) * width
    return pl.pallas_call(
        functools.partial(mix_kernel, plan, (frames, rows, width)),
        grid_spec=pltpu.PrefetchScalarGridSpec(
            num_scalar_prefetch=1,
            grid=(plan.steps,),
            in_specs=in_specs,
            out_specs=body,
        ),
        out_shape=jax.ShapeDtypeStruct(queries.shape, jnp.bfloat16),
        input_output_aliases=aliases,
        compiler_params=pltpu.CompilerParams(
            dimension_semantics=("arbitrary",), vmem_limit_bytes=32 << 20
        ),
        cost_estimate=pl.CostEstimate(
            flops=2 * tokens * plan.blocks * LANES * LANES * 2,
            bytes_accessed=8 * tokens * plan.blocks * LANES,
            transcendentals=tokens * plan.blocks * LANES,
        ),
        name="mix",
    )(half, *operands)


def swap(array, axis, bit):
    n = lax.axis_size(axis)
    return lax.ppermute(array, axis, [(i, i ^ bit) for i in range(n)])


def per_device(queries, keys, values, gate, conv_weight):
    frames, rows, width, channels = queries.shape
    tokens = rows * width
    n_row, n_frame = lax.axis_size("row"), lax.axis_size("frame")
    me_row, me_frame = lax.axis_index("row"), lax.axis_index("frame")
    f32, bf16 = jnp.float32, jnp.bfloat16

    top = n_row // 2
    plan = Plan(channels, 2)
    own = (me_row // top).astype(jnp.int32).reshape(1)
    other = 1 - own

    ring = [(i, i + 1) for i in range(n_row - 1)]
    up = lax.ppermute(queries[:, rows - 1 :], "row", ring)
    down = lax.ppermute(queries[:, :1], "row", [(j, i) for i, j in ring])

    keys = keys.reshape(frames, tokens, channels)
    values = values.reshape(frames, tokens, channels)
    send = sums(plan, other, keys, values, bf16)
    got = swap(send, "row", top)
    mine = sums(plan, own, keys, values, f32) + got.astype(f32)

    total = jnp.sum(mine, axis=0)
    neighbour = swap(total.astype(bf16), "frame", 1).astype(f32)
    second = (me_frame % 2) == 1
    before = jnp.where(second, neighbour, 0.0)
    running = total + neighbour
    pairs = n_frame // 2
    reach = 1
    while reach < pairs:
        hop = [(i, i + 2 * reach) for i in range(n_frame - 2 * reach)]
        earlier = lax.ppermute(running.astype(bf16), "frame", hop).astype(f32)
        before = before + earlier
        running = running + earlier
        reach *= 2
    states = before[None] + jnp.cumsum(mine, axis=0)
    bit = 1
    while bit < top:
        states = states + swap(states.astype(bf16), "row", bit).astype(f32)
        bit *= 2
    states = states.astype(bf16)
    others = swap(states, "row", top)

    weight = conv_weight.reshape(9, channels)
    out = mix(plan, own, states, queries, up, down, gate, weight, None)
    return mix(plan, other, others, queries, up, down, gate, weight, out)


def solution(mesh):
    spec = P("frame", "row", None, None)
    return jax.shard_map(
        per_device,
        mesh=mesh,
        in_specs=(spec, spec, spec, spec, P()),
        out_specs=spec,
        check_vma=False,
    )
```

time: 308 us -> 76.3 us (0.25)
  blocking collectives: 96.2 us -> 0 us
  other arithmetic: 86.6 us -> 1.8 us
  matrix products: 71.2 us -> 0 us
  starting transfers between devices: 4.67 us -> 21.6 us
  Pallas kernels: 0 us -> 16.4 us
  between operations: 15 us -> 0.11 us
  waiting for transfers between devices: 21.8 us -> 29 us
  local copies, waits for them, and re-layouts: 11.7 us -> 7.03 us
    dot_general x8 -> x0, matrix products: 71.2 us -> none  [the longest x2 40.7 us: read_frame(): numer = jnp.dot(qf, blocked, precision=lax.Precision.HIGHEST)]
    all_gather x3 -> x0, blocking collectives: 52.2 us -> none  [the longest x1 24.5 us: per_device(): lax.all_gather(states, 'row', axis=2, tiled=True)]
    unnamed x2 -> x0, blocking collectives: 44 us -> none
    mul x2 -> x0, other arithmetic: 31.3 us -> none  [read_frame(): blocked = jnp.tile(state, (HEADS, 1)) * block]
    convert_element_type x4, other arithmetic: 26.4 us -> 0.74 us  [the longest x2 0.67 us: per_device(): earlier = lax.ppermute(running.astype(bf16), 'frame', hop).astype(f32)]
    reduce_sum x5 -> x1, other arithmetic: 19 us -> 0.04 us  [per_device(): total = jnp.sum(mine, axis=0)]
    ppermute x2 -> x8, starting transfers between devices: 4.66 us -> 21.6 us  [the longest x2 9.64 us: per_device(): earlier = lax.ppermute(running.astype(bf16), 'frame', hop).astype(f32)]
    pallas_call x0 -> x4, Pallas kernels: none -> 16.4 us  [the longest x2 13.8 us: mix(): pl.pallas_call(functools.partial(mix_kernel, plan, (frames, rows, width))...]
  transfers between devices with their start and end apart: 3 -> 8, of which waited for: 2 -> 4; matrix products, arithmetic and copies ran while one was open for 1% -> 4% of each run, Pallas kernels for 0% -> 11%
where the time goes in v1:
time: 76.3 us; the launch traced here: 75.9 us
  waiting for transfers between devices  29 us (38%)
  starting transfers between devices  21.6 us (28%)
  Pallas kernels  16.4 us (21%)
  local copies, waits for them, and re-layouts  7.03 us (9%)
  other arithmetic  1.8 us (2%)
    ppermute x4, waiting for transfers between devices, swap(): return lax.ppermute(array, axis, [(i, i ^ bit) for i in range(n)])  27 us
    pallas_call x2, Pallas kernels, mix(): pl.pallas_call(functools.partial(mix_kernel, plan, (frames, rows, width))...  13.8 us
    ppermute x2, starting transfers between devices, per_device(): earlier = lax.ppermute(running.astype(bf16), 'frame', hop).astype(f32)  9.64 us
    ppermute x1, starting transfers between devices, per_device(): up = lax.ppermute(queries[:, rows - 1:], 'row', ring)  5.36 us
    ppermute x4, starting transfers between devices, swap(): return lax.ppermute(array, axis, [(i, i ^ bit) for i in range(n)])  5.32 us
    unnamed x14, local copies, waits for them, and re-layouts  5.01 us
    pallas_call x2, Pallas kernels, sums(): pl.pallas_call(functools.partial(sums_kernel, plan, frames), grid_spec=pl...  2.59 us
    ppermute x2, waiting for transfers between devices, per_device(): earlier = lax.ppermute(running.astype(bf16), 'frame', hop).astype(f32)  2 us
  transfers between devices with their start and end apart: 8, of which 4 were waited for; matrix products, arithmetic and copies ran while one was open for 4% of the time, Pallas kernels for 11%

profile of v1, /device:TPU:0, one launch (start us, length us, event | category | flops | bytes accessed | tf_op | source)
XLA Modules:
  0.0 75.9 jit_solution(18004147431910544657)
XLA Ops:
  0.0 0.0 copy-start.1
  0.0 1.7 %copy-done.1 = bf16[2,4,64,2240]{3,2,1,0:T(8,128)(2,1)S(1)} copy-done((bf16[2,4,64,2240]{3,2,1,0:T(8,128)(2,1)S(1)}, bf16[2,4,64,2240]{3,2,1,0:T(8,128)(2,1)}, u32[]{:S(2)}) %copy-start.1) | copy-done | bytes 2293784
  1.7 0.0 copy-start.3
  1.7 1.7 %copy-done.3 = bf16[2,4,64,2240]{3,2,1,0:T(8,128)(2,1)S(1)} copy-done((bf16[2,4,64,2240]{3,2,1,0:T(8,128)(2,1)S(1)}, bf16[2,4,64,2240]{3,2,1,0:T(8,128)(2,1)}, u32[]{:S(2)}) %copy-start.3) | copy-done | bytes 2293784
  3.3 0.0 copy-start.2
  3.3 1.3 %sums.3 = bf16[2,304,128]{2,1,0:T(8,128)(2,1)S(1)} custom-call(s32[1]{0:T(128)S(6)} %sub.8.half_ref, bf16[2,256,2240]{2,1,0:T(8,128)(2,1)S(1)} %bitcast.3, bf16[2,256,2240]{2,1,0:T(8,128)(2,1)S(1)} %bitcast.5), custom_call_target="tpu_custom_call" | custom-call | flops 150994944 | bytes 2359296 | tf_op jit(solution)/shard_map/sums/pallas_call | solution.py:76
  4.6 0.0 copy-start
  4.6 3.0 %collective-permute-start = (bf16[2,304,128]{2,1,0:T(8,128)(2,1)S(1)}, bf16[2,304,128]{2,1,0:T(8,128)(2,1)S(1)}, u32[]{:S(2)}, u32[]{:S(2)}) collective-permute-start(bf16[2,304,128]{2,1,0:T(8,128)(2,1)S(1)} %sums.3), channel_id=1, source_target_pairs={{0,2},{1,3},{2,0},{3,1},{4,6},{5,7},{6,4},{7,5},{8,10},{9,11},{10,... | collective-permute-start | bytes 466952 | tf_op jit(solution)/shard_map/ppermute | solution.py:200
  7.7 0.0 copy-done.2
  7.7 1.3 %sums.2 = f32[2,304,128]{2,1,0:T(8,128)S(1)} custom-call(s32[1]{0:T(128)} %bitcast.half_ref, bf16[2,256,2240]{2,1,0:T(8,128)(2,1)S(1)} %bitcast.4, bf16[2,256,2240]{2,1,0:T(8,128)(2,1)S(1)} %bitcast.6), custom_call_target="tpu_custom_call" | custom-call | flops 150994944 | bytes 2359296 | tf_op jit(solution)/shard_map/sums/pallas_call | solution.py:76
  9.0 2.7 %collective-permute-done = bf16[2,304,128]{2,1,0:T(8,128)(2,1)S(1)} collective-permute-done((bf16[2,304,128]{2,1,0:T(8,128)(2,1)S(1)}, bf16[2,304,128]{2,1,0:T(8,128)(2,1)S(1)}, u32[]{:S(2)}, u32[]{:S(2)}) %collective-permute-start) | collective-permute-done | bytes 155680 | tf_op jit(solution)/shard_map/ppermute | solution.py:200
  11.8 0.1 collective-permute-start.1
  11.8 1.3 %collective-permute-done.1 = bf16[304,128]{1,0:T(8,128)(2,1)S(1)} collective-permute-done((bf16[304,128]{1,0:T(8,128)(2,1)S(1)}, bf16[304,128]{1,0:T(8,128)(2,1)S(1)}, u32[]{:S(2)}, u32[]{:S(2)}) %collective-permute-start.1) | collective-permute-done | bytes 77856 | tf_op jit(solution)/shard_map/ppermute | solution.py:200
  13.1 3.7 %collective-permute-start.2 = (bf16[304,128]{1,0:T(8,128)(2,1)S(1)}, bf16[304,128]{1,0:T(8,128)(2,1)S(1)}, u32[]{:S(2)}, u32[]{:S(2)}) collective-permute-start(bf16[304,128]{1,0:T(8,128)(2,1)S(1)} %fusion.4), channel_id=1, source_target_pairs={{0,8},{4,12},{8,16},{12,20},{16,24},{20,28},{1,9},{5,13},{9,17},{1... | collective-permute-start | bytes 233480 | tf_op jit(solution)/shard_map/ppermute | solution.py:234
  16.8 2.0 %collective-permute-done.2 = bf16[304,128]{1,0:T(8,128)(2,1)S(1)} collective-permute-done((bf16[304,128]{1,0:T(8,128)(2,1)S(1)}, bf16[304,128]{1,0:T(8,128)(2,1)S(1)}, u32[]{:S(2)}, u32[]{:S(2)}) %collective-permute-start.2) | collective-permute-done | bytes 77856 | tf_op jit(solution)/shard_map/ppermute | solution.py:234
  18.8 0.0 copy-start.6
  18.8 0.7 fusion.3
  19.5 5.9 %collective-permute-start.3 = (bf16[304,128]{1,0:T(8,128)(2,1)}, bf16[304,128]{1,0:T(8,128)(2,1)}, u32[]{:S(2)}, u32[]{:S(2)}) collective-permute-start(bf16[304,128]{1,0:T(8,128)(2,1)} %fusion.3), channel_id=1, source_target_pairs={{0,16},{4,20},{8,24},{12,28},{1,17},{5,21},{9,25},{13,29},{2,18},{... | collective-permute-start | bytes 233480 | tf_op jit(solution)/shard_map/ppermute | solution.py:234
  25.4 0.0 copy-done
  25.4 1.1 %fusion.5 = (bf16[2,1,64,2240]{3,2,1,0:T(8,128)(2,1)}, bf16[2,1,64,2240]{3,2,1,0:T(8,128)(2,1)}) fusion(bf16[2,4,64,2240]{3,2,1,0:T(8,128)(2,1)S(1)} %copy-done), kind=kLoop, calls=%fused_computation.12 | loop fusion | bytes 2293760 | tf_op jit(solution)/shard_map/slice | solution.py:217
  26.5 0.0 copy-done.6
  26.5 1.3 %collective-permute-start.7 = (bf16[2,1,64,2240]{3,2,1,0:T(8,128)(2,1)}, bf16[2,1,64,2240]{3,2,1,0:T(8,128)(2,1)S(1)}, u32[]{:S(2)}, u32[]{:S(2)}) collective-permute-start(bf16[2,1,64,2240]{3,2,1,0:T(8,128)(2,1)} %get-tuple-element.5), channel_id=1, source_target_pairs={{1,0},{2,1},{3,2},{5,4},{6,5},{7,6},{9,8},{10,9},{11,10},{13,12},{... | collective-permute-start | bytes 1720328 | tf_op jit(solution)/shard_map/ppermute | solution.py:217
  27.8 5.4 %collective-permute-start.6 = (bf16[2,1,64,2240]{3,2,1,0:T(8,128)(2,1)}, bf16[2,1,64,2240]{3,2,1,0:T(8,128)(2,1)}, u32[]{:S(2)}, u32[]{:S(2)}) collective-permute-start(bf16[2,1,64,2240]{3,2,1,0:T(8,128)(2,1)} %get-tuple-element.6), channel_id=1, source_target_pairs={{0,1},{1,2},{2,3},{4,5},{5,6},{6,7},{8,9},{9,10},{10,11},{12,13},{... | collective-permute-start | bytes 1720328 | tf_op jit(solution)/shard_map/ppermute | solution.py:216
  33.2 0.0 collective-permute-done.3
  33.2 1.0 %fusion.2 = f32[304,128]{1,0:T(8,128)S(1)} fusion(bf16[304,128]{1,0:T(8,128)(2,1)} %copy-done.6, bf16[304,128]{1,0:T(8,128)(2,1)S(1)} %collective-permute-done.1, bf16[304,128]{1,0:T(8,128)(2,1)} %collective-permute-done.3, pred[]{:T(512)S(6)} %eq.5), kind=kLoop, calls=%fused_computation.9 | loop fusion | flops 233472 | bytes 389121 | tf_op jit(solution)/shard_map/add | solution.py:235
  34.1 0.1 add_convert_fusion.1
  34.2 1.7 %collective-permute-start.4 = (bf16[2,304,128]{2,1,0:T(8,128)(2,1)S(1)}, bf16[2,304,128]{2,1,0:T(8,128)(2,1)S(1)}, u32[]{:S(2)}, u32[]{:S(2)}) collective-permute-start(bf16[2,304,128]{2,1,0:T(8,128)(2,1)S(1)} %get-tuple-element.7), channel_id=1, source_target_pairs={{0,1},{1,0},{2,3},{3,2},{4,5},{5,4},{6,7},{7,6},{8,9},{9,8},{10,11... | collective-permute-start | bytes 466952 | tf_op jit(solution)/shard_map/ppermute | solution.py:200
  35.9 23.0 %collective-permute-done.4 = bf16[2,304,128]{2,1,0:T(8,128)(2,1)S(1)} collective-permute-done((bf16[2,304,128]{2,1,0:T(8,128)(2,1)S(1)}, bf16[2,304,128]{2,1,0:T(8,128)(2,1)S(1)}, u32[]{:S(2)}, u32[]{:S(2)}) %collective-permute-start.4) | collective-permute-done | bytes 155680 | tf_op jit(solution)/shard_map/ppermute | solution.py:200
  58.9 0.1 add_convert_fusion.s_ref
  58.9 0.5 collective-permute-start.5
  59.5 0.9 %reshape.16.w_ref = f32[9,2240]{1,0:T(8,128)S(1)} reshape(f32[3,3,2240]{2,1,0:T(4,128)} %param.9) | data formatting | bytes 161280 | tf_op jit(solution)/shard_map/reshape | solution.py:246
  60.4 0.0 collective-permute-done.7.down_ref
  60.4 0.0 collective-permute-done.6.up_ref
  60.4 0.0 copy-start.4
  60.4 1.7 %copy-done.4 = bf16[2,4,64,2240]{3,2,1,0:T(8,128)(2,1)S(1)} copy-done((bf16[2,4,64,2240]{3,2,1,0:T(8,128)(2,1)S(1)}, bf16[2,4,64,2240]{3,2,1,0:T(8,128)(2,1)}, u32[]{:S(2)}) %copy-start.4) | copy-done | bytes 2293784
  62.1 0.0 copy-start.5
  62.1 7.0 %mix.2.rest_0_ = bf16[2,4,64,2240]{3,2,1,0:T(8,128)(2,1)} custom-call(s32[1]{0:T(128)} %bitcast.half_ref, bf16[2,304,128]{2,1,0:T(8,128)(2,1)S(1)} %add_convert_fusion.s_ref, bf16[2,4,64,2240]{3,2,1,0:T(8,128)(2,1)S(1)} %copy-done, bf16[2,1,64,2240]{3,2,1,0:T(8,128)(2,1)} %collective-permute-done.6.up_ref, ...), custom_call_target="tpu_custom_call" | custom-call | flops 452984832 | bytes 7077888 | tf_op jit(solution)/shard_map/mix/pallas_call | solution.py:176
  69.1 0.0 collective-permute-done.5.s_ref
  69.1 0.0 copy-done.5
  69.1 6.8 %mix.3 = bf16[2,4,64,2240]{3,2,1,0:T(8,128)(2,1)} custom-call(s32[1]{0:T(128)S(6)} %sub.8.half_ref, bf16[2,304,128]{2,1,0:T(8,128)(2,1)S(1)} %collective-permute-done.5.s_ref, bf16[2,4,64,2240]{3,2,1,0:T(8,128)(2,1)S(1)} %copy-done, bf16[2,1,64,2240]{3,2,1,0:T(8,128)(2,1)} %collective-permute-done.6.up_ref, ...), custom_call_target="tpu_custom_call", output_to_operand_aliasing={{}: (7, {})} | custom-call | flops 452984832 | bytes 7077888 | tf_op jit(solution)/shard_map/mix/pallas_call | solution.py:176
  (3 shorter events, 0.1 us)
Async XLA Ops:
  0.0 1.7 %copy-start.1 = (bf16[2,4,64,2240]{3,2,1,0:T(8,128)(2,1)S(1)}, bf16[2,4,64,2240]{3,2,1,0:T(8,128)(2,1)}, u32[]{:S(2)}) copy-start(bf16[2,4,64,2240]{3,2,1,0:T(8,128)(2,1)} %param.6) | copy-start | bytes 6881284
  1.7 1.7 %copy-start.3 = (bf16[2,4,64,2240]{3,2,1,0:T(8,128)(2,1)S(1)}, bf16[2,4,64,2240]{3,2,1,0:T(8,128)(2,1)}, u32[]{:S(2)}) copy-start(bf16[2,4,64,2240]{3,2,1,0:T(8,128)(2,1)} %param.7) | copy-start | bytes 6881284
  3.3 4.4 %copy-start.2 = (bf16[2,4,64,2240]{3,2,1,0:T(8,128)(2,1)S(1)}, bf16[2,4,64,2240]{3,2,1,0:T(8,128)(2,1)}, u32[]{:S(2)}) copy-start(bf16[2,4,64,2240]{3,2,1,0:T(8,128)(2,1)} %param.6) | copy-start | bytes 6881284
  4.6 20.8 %copy-start = (bf16[2,4,64,2240]{3,2,1,0:T(8,128)(2,1)S(1)}, bf16[2,4,64,2240]{3,2,1,0:T(8,128)(2,1)}, u32[]{:S(2)}) copy-start(bf16[2,4,64,2240]{3,2,1,0:T(8,128)(2,1)} %q_ref.3) | copy-start | bytes 6881284
  4.6 7.1 %collective-permute-start = (bf16[2,304,128]{2,1,0:T(8,128)(2,1)S(1)}, bf16[2,304,128]{2,1,0:T(8,128)(2,1)S(1)}, u32[]{:S(2)}, u32[]{:S(2)}) collective-permute-start(bf16[2,304,128]{2,1,0:T(8,128)(2,1)S(1)} %sums.3), channel_id=1, source_target_pairs={{0,2},{1,3},{2,0},{3,1},{4,6},{5,7},{6,4},{7,5},{8,10},{9,11},{10,... | collective-permute-start | bytes 466952 | tf_op jit(solution)/shard_map/ppermute | solution.py:200
  11.8 1.3 %collective-permute-start.1 = (bf16[304,128]{1,0:T(8,128)(2,1)S(1)}, bf16[304,128]{1,0:T(8,128)(2,1)S(1)}, u32[]{:S(2)}, u32[]{:S(2)}) collective-permute-start(bf16[304,128]{1,0:T(8,128)(2,1)S(1)} %convert_element_type.31), channel_id=1, source_target_pairs={{0,4},{4,0},{8,12},{12,8},{16,20},{20,16},{24,28},{28,24},{1,5},{5... | collective-permute-start | bytes 233480 | tf_op jit(solution)/shard_map/ppermute | solution.py:200
  13.1 5.7 %collective-permute-start.2 = (bf16[304,128]{1,0:T(8,128)(2,1)S(1)}, bf16[304,128]{1,0:T(8,128)(2,1)S(1)}, u32[]{:S(2)}, u32[]{:S(2)}) collective-permute-start(bf16[304,128]{1,0:T(8,128)(2,1)S(1)} %fusion.4), channel_id=1, source_target_pairs={{0,8},{4,12},{8,16},{12,20},{16,24},{20,28},{1,9},{5,13},{9,17},{1... | collective-permute-start | bytes 233480 | tf_op jit(solution)/shard_map/ppermute | solution.py:234
  18.8 7.7 %copy-start.6 = (bf16[304,128]{1,0:T(8,128)(2,1)}, bf16[304,128]{1,0:T(8,128)(2,1)S(1)}, u32[]{:S(2)}) copy-start(bf16[304,128]{1,0:T(8,128)(2,1)S(1)} %collective-permute-done.2) | copy-start | bytes 233476
  19.5 13.7 %collective-permute-start.3 = (bf16[304,128]{1,0:T(8,128)(2,1)}, bf16[304,128]{1,0:T(8,128)(2,1)}, u32[]{:S(2)}, u32[]{:S(2)}) collective-permute-start(bf16[304,128]{1,0:T(8,128)(2,1)} %fusion.3), channel_id=1, source_target_pairs={{0,16},{4,20},{8,24},{12,28},{1,17},{5,21},{9,25},{13,29},{2,18},{... | collective-permute-start | bytes 233480 | tf_op jit(solution)/shard_map/ppermute | solution.py:234
  26.5 33.9 %collective-permute-start.7 = (bf16[2,1,64,2240]{3,2,1,0:T(8,128)(2,1)}, bf16[2,1,64,2240]{3,2,1,0:T(8,128)(2,1)S(1)}, u32[]{:S(2)}, u32[]{:S(2)}) collective-permute-start(bf16[2,1,64,2240]{3,2,1,0:T(8,128)(2,1)} %get-tuple-element.5), channel_id=1, source_target_pairs={{1,0},{2,1},{3,2},{5,4},{6,5},{7,6},{9,8},{10,9},{11,10},{13,12},{... | collective-permute-start | bytes 1720328 | tf_op jit(solution)/shard_map/ppermute | solution.py:217
  27.8 32.6 %collective-permute-start.6 = (bf16[2,1,64,2240]{3,2,1,0:T(8,128)(2,1)}, bf16[2,1,64,2240]{3,2,1,0:T(8,128)(2,1)}, u32[]{:S(2)}, u32[]{:S(2)}) collective-permute-start(bf16[2,1,64,2240]{3,2,1,0:T(8,128)(2,1)} %get-tuple-element.6), channel_id=1, source_target_pairs={{0,1},{1,2},{2,3},{4,5},{5,6},{6,7},{8,9},{9,10},{10,11},{12,13},{... | collective-permute-start | bytes 1720328 | tf_op jit(solution)/shard_map/ppermute | solution.py:216
  34.2 24.7 %collective-permute-start.4 = (bf16[2,304,128]{2,1,0:T(8,128)(2,1)S(1)}, bf16[2,304,128]{2,1,0:T(8,128)(2,1)S(1)}, u32[]{:S(2)}, u32[]{:S(2)}) collective-permute-start(bf16[2,304,128]{2,1,0:T(8,128)(2,1)S(1)} %get-tuple-element.7), channel_id=1, source_target_pairs={{0,1},{1,0},{2,3},{3,2},{4,5},{5,4},{6,7},{7,6},{8,9},{9,8},{10,11... | collective-permute-start | bytes 466952 | tf_op jit(solution)/shard_map/ppermute | solution.py:200
  58.9 10.1 %collective-permute-start.5 = (bf16[2,304,128]{2,1,0:T(8,128)(2,1)S(1)}, bf16[2,304,128]{2,1,0:T(8,128)(2,1)S(1)}, u32[]{:S(2)}, u32[]{:S(2)}) collective-permute-start(bf16[2,304,128]{2,1,0:T(8,128)(2,1)S(1)} %add_convert_fusion.s_ref), channel_id=1, source_target_pairs={{0,2},{1,3},{2,0},{3,1},{4,6},{5,7},{6,4},{7,5},{8,10},{9,11},{10,... | collective-permute-start | bytes 466952 | tf_op jit(solution)/shard_map/ppermute | solution.py:200
  60.4 1.7 %copy-start.4 = (bf16[2,4,64,2240]{3,2,1,0:T(8,128)(2,1)S(1)}, bf16[2,4,64,2240]{3,2,1,0:T(8,128)(2,1)}, u32[]{:S(2)}) copy-start(bf16[2,4,64,2240]{3,2,1,0:T(8,128)(2,1)} %g_ref.3) | copy-start | bytes 6881284
  62.1 7.0 %copy-start.5 = (bf16[2,4,64,2240]{3,2,1,0:T(8,128)(2,1)S(1)}, bf16[2,4,64,2240]{3,2,1,0:T(8,128)(2,1)}, u32[]{:S(2)}) copy-start(bf16[2,4,64,2240]{3,2,1,0:T(8,128)(2,1)} %g_ref.3) | copy-start | bytes 6881284

commit v2 on v1

v2 whole, which is shorter than its diff:
```python
import functools

import jax
import jax.numpy as jnp
from jax import lax
from jax.experimental import pallas as pl
from jax.experimental.pallas import tpu as pltpu
from jax.sharding import PartitionSpec as P

HEAD_DIM = 32
LANES = 128
GROUP = LANES // HEAD_DIM
Z_ALIGN = 16
MARGIN = 8
CHUNK = 16
PARTS = 2
SUMS_LIMIT = 60 << 20
READY_LIMIT = 52 << 20
MIX_LIMIT = 40 << 20


def ceil_div(a, b):
    return -(-a // b)


class Plan:
    def __init__(self, channels, halves):
        total = ceil_div(channels, LANES)
        self.channels = channels
        self.halves = halves
        self.blocks = ceil_div(total, halves)
        self.per = max(p for p in (1, 2, 3) if self.blocks % p == 0)
        self.steps = self.blocks // self.per
        self.z_row = self.blocks * HEAD_DIM
        self.rows = self.z_row + ceil_div(self.blocks, Z_ALIGN) * Z_ALIGN
        self.width = self.per * LANES


def same_head():
    row = lax.broadcasted_iota(jnp.int32, (LANES, LANES), 0) // HEAD_DIM
    col = lax.broadcasted_iota(jnp.int32, (LANES, LANES), 1) // HEAD_DIM
    return row == col


def sums_kernel(
    plan,
    own_ref,
    odd_ref,
    k_hbm,
    v_hbm,
    q_hbm,
    send_ref,
    mine_ref,
    far_ref,
    *rest,
):
    *near_refs, k_ref, v_ref, acc_ref, sems, edge_sems = rest
    frames, tokens, channels = k_ref.shape
    rows = q_hbm.shape[1]
    part = tokens // PARTS
    odd = odd_ref[0]
    copies = []
    for f in range(frames):
        for p in range(PARTS):
            at = (f, pl.ds(p * part, part))
            copies.append(
                [
                    pltpu.make_async_copy(k_hbm.at[at], k_ref.at[at], sems.at[0, f, p]),
                    pltpu.make_async_copy(v_hbm.at[at], v_ref.at[at], sems.at[1, f, p]),
                ]
            )
    edges = [
        pltpu.make_async_copy(
            q_hbm.at[:, pl.ds((rows - 1) * (1 - odd), 1)], near, edge_sems.at[f]
        )
        for f, near in enumerate(near_refs)
    ]
    edges.append(
        pltpu.make_async_copy(
            q_hbm.at[:, pl.ds((rows - 1) * odd, 1)], far_ref, edge_sems.at[1]
        )
    )
    for pair in copies:
        for copy in pair:
            copy.start()
    for edge in edges:
        edge.start()

    mask = same_head()
    acc_ref[:, :, plan.z_row :, :] = jnp.zeros(
        (plan.halves, frames, plan.rows - plan.z_row, LANES), jnp.float32
    )
    for f in range(frames):
        for pair in copies[f * PARTS : (f + 1) * PARTS]:
            for copy in pair:
                copy.wait()
        for index in range(ceil_div(channels, LANES)):
            half, block = divmod(index, plan.blocks)
            lanes = slice(index * LANES, min((index + 1) * LANES, channels))
            kf = jnp.maximum(k_ref[f, :, lanes], 0)
            v = v_ref[f, :, lanes]
            if kf.shape[1] < LANES:
                rest = jnp.zeros((tokens, LANES - kf.shape[1]), kf.dtype)
                kf = jnp.concatenate([kf, rest], axis=1)
                v = jnp.concatenate([v, rest], axis=1)
            full = lax.dot_general(
                kf, v, (((0,), (0,)), ((), ())), preferred_element_type=jnp.float32
            )
            full = jnp.where(mask, full, 0.0)
            state = full.reshape(GROUP, HEAD_DIM, LANES).sum(axis=0)
            norm = jnp.sum(kf.astype(jnp.float32), axis=0, keepdims=True)
            acc_ref[half, f, block * HEAD_DIM : (block + 1) * HEAD_DIM, :] = state
            acc_ref[half, f, plan.z_row + block : plan.z_row + block + 1, :] = norm
    own = own_ref[0]
    mine_ref[...] = acc_ref[own]
    send_ref[...] = acc_ref[1 - own].astype(send_ref.dtype)
    for edge in edges:
        edge.wait()


def sums(plan, own, odd, keys, values, queries):
    frames, tokens, channels = keys.shape
    _, rows, width, _ = queries.shape
    scalar = pl.BlockSpec(memory_space=pltpu.SMEM)
    anywhere = pl.BlockSpec(memory_space=pl.ANY)
    whole = pl.BlockSpec(memory_space=pltpu.VMEM)
    state = (frames, plan.rows, LANES)
    return pl.pallas_call(
        functools.partial(sums_kernel, plan),
        in_specs=[scalar, scalar, anywhere, anywhere, anywhere],
        out_specs=[whole] * 4,
        scratch_shapes=[
            pltpu.VMEM((frames, tokens, channels), keys.dtype),
            pltpu.VMEM((frames, tokens, channels), values.dtype),
            pltpu.VMEM((plan.halves, frames, plan.rows, LANES), jnp.float32),
            pltpu.SemaphoreType.DMA((2, frames, PARTS)),
            pltpu.SemaphoreType.DMA((2,)),
        ],
        out_shape=[
            pltpu.VMEM(state, jnp.bfloat16),
            pltpu.VMEM(state, jnp.float32),
            pltpu.VMEM((frames, 1, width, channels), queries.dtype),
        ]
        + [pltpu.VMEM((frames, 1, width, channels), queries.dtype)],
        compiler_params=pltpu.CompilerParams(vmem_limit_bytes=SUMS_LIMIT),
        cost_estimate=pl.CostEstimate(
            flops=2 * frames * tokens * channels * LANES,
            bytes_accessed=4 * frames * tokens * channels,
            transcendentals=0,
        ),
        name="sums",
    )(own, odd, keys, values, queries)


def ready_kernel(plan, q_ref, g_ref, qf_ref, sg_ref):
    step = pl.program_id(0)
    frames, tokens = qf_ref.shape[1:3]
    lane = lax.broadcasted_iota(jnp.int32, (1, LANES), 1)
    for b in range(plan.per):
        lanes = slice(b * LANES, (b + 1) * LANES)
        block = step * plan.per + b
        live = lane + block * LANES < plan.channels
        q = q_ref[:, :, :, lanes].reshape(frames, tokens, LANES)
        qf_ref[block] = jnp.where(live, jnp.maximum(q, 0), jnp.zeros_like(q))
        g = 0.5 * g_ref[:, :, :, lanes].astype(jnp.float32).reshape(frames, tokens, LANES)
        sg_ref[block] = g + g * jnp.tanh(g)


def ready(plan, queries, gate):
    frames, rows, width, channels = queries.shape
    body = pl.BlockSpec((frames, rows, width, plan.width), lambda i: (0, 0, 0, i))
    whole = pl.BlockSpec(memory_space=pltpu.VMEM)
    shape = (plan.halves * plan.blocks, frames, rows * width, LANES)
    return pl.pallas_call(
        functools.partial(ready_kernel, plan),
        grid=(plan.halves * plan.steps,),
        in_specs=[body, body],
        out_specs=[whole, whole],
        out_shape=[pltpu.VMEM(shape, jnp.bfloat16), pltpu.VMEM(shape, jnp.float32)],
        compiler_params=pltpu.CompilerParams(
            dimension_semantics=("arbitrary",), vmem_limit_bytes=READY_LIMIT
        ),
        cost_estimate=pl.CostEstimate(
            flops=8 * frames * rows * width * channels,
            bytes_accessed=10 * frames * rows * width * channels,
            transcendentals=frames * rows * width * channels,
        ),
        name="ready",
    )(queries, gate)


def mix_kernel(plan, shape, half_ref, odd_ref, s_ref, qf_ref, sg_ref, w_ref, far_ref, *rest):
    o_ref, att_ref = rest[-2:]
    near_ref = rest[0]
    frames, rows, width = shape
    step = pl.program_id(0)
    ones = same_head().astype(jnp.bfloat16)
    nothing = jnp.zeros_like(ones)
    lower = jnp.concatenate([nothing, ones], axis=1)
    z_iota = lax.broadcasted_iota(jnp.int32, (plan.rows - plan.z_row, LANES), 0)
    lane = lax.broadcasted_iota(jnp.int32, (1, LANES), 1)
    first = (half_ref[0] * plan.steps + step) * plan.width

    half_block = half_ref[0] * plan.blocks
    near_row = (rows + 1) * (1 - odd_ref[0])

    @pl.when(step == 0)
    def _():
        side = jnp.zeros(att_ref.shape[:2] + (MARGIN, LANES), jnp.float32)
        att_ref[:, :, :MARGIN, :] = side
        att_ref[:, :, MARGIN + width :, :] = side

    for f in range(frames):
        zs = s_ref[f, plan.z_row :, :].astype(jnp.float32)
        for b in range(plan.per):
            slot = (f * plan.per + b) % att_ref.shape[0]
            lanes = slice(b * LANES, (b + 1) * LANES)
            block = step * plan.per + b
            live = lane + (first + b * LANES) < plan.channels
            state = s_ref[f, pl.ds(pl.multiple_of(block * HEAD_DIM, HEAD_DIM), HEAD_DIM), :]
            numer = jnp.concatenate([state] * GROUP, axis=0) * ones
            weights = jnp.concatenate(
                [jnp.concatenate([numer, nothing], axis=1), lower], axis=0
            )
            z = jnp.sum(jnp.where(z_iota == block, zs, 0.0), axis=0, keepdims=True)
            z = z.astype(jnp.bfloat16)
            edge = jnp.concatenate(
                [
                    near_ref[f, :, :, lanes].reshape(width, LANES),
                    far_ref[f, :, :, lanes].reshape(width, LANES),
                ],
                axis=0,
            )
            edge = jnp.where(live, jnp.maximum(edge, 0), jnp.zeros_like(edge))
            qf = jnp.concatenate([qf_ref[half_block + block, f], edge], axis=0)
            both = jnp.dot(
                jnp.concatenate([qf, qf * z], axis=1),
                weights,
                preferred_element_type=jnp.float32,
            )
            att = both[:, :LANES] * pltpu.reciprocal(both[:, LANES:] + 1e-6, approx=True)
            att = att.reshape(rows + 2, width, LANES)
            att_ref[slot, 1 : rows + 1, MARGIN : MARGIN + width, :] = att[:rows]
            att_ref[slot, near_row, MARGIN : MARGIN + width, :] = att[rows]
            att_ref[slot, rows + 1 - near_row, MARGIN : MARGIN + width, :] = att[rows + 1]
            taps = [[w_ref[a, c, lanes] for c in range(3)] for a in range(3)]
            for start in range(0, width, CHUNK):
                near = [
                    [
                        att_ref[slot, r, pl.ds(MARGIN - 1 + c + start, CHUNK), :]
                        for c in range(3)
                    ]
                    for r in range(rows + 2)
                ]
                for r in range(rows):
                    conv = None
                    for a in range(3):
                        for c in range(3):
                            term = near[r + a][c] * taps[a][c]
                            conv = term if conv is None else conv + term
                    at = r * width + start
                    mixed = conv * sg_ref[half_block + block, f, at : at + CHUNK, :]
                    o_ref[f, r, start : start + CHUNK, lanes] = mixed.astype(o_ref.dtype)


def mix(plan, shape, half, odd, states, qf, near, far, sg, weight, earlier):
    frames, rows, width, channels = shape
    col = lambda i, half, odd: (0, 0, 0, half[0] * plan.steps + i)
    body = pl.BlockSpec((frames, rows, width, plan.width), col)
    edge = lambda n: pl.BlockSpec((n, 1, width, plan.width), col)
    whole = pl.BlockSpec(memory_space=pltpu.VMEM)
    in_specs = [
        whole,
        whole,
        whole,
        pl.BlockSpec((3, 3, plan.width), lambda i, half, odd: (0, 0, half[0] * plan.steps + i)),
        edge(frames),
        edge(frames),
    ]
    operands = [states, qf, sg, weight, far, *near]
    aliases = {}
    if earlier is not None:
        in_specs.append(pl.BlockSpec(memory_space=pl.ANY))
        operands.append(earlier)
        aliases = {8: 0}
    tokens = frames * (rows + 2) * width
    return pl.pallas_call(
        functools.partial(mix_kernel, plan, (frames, rows, width)),
        grid_spec=pltpu.PrefetchScalarGridSpec(
            num_scalar_prefetch=2,
            grid=(plan.steps,),
            in_specs=in_specs,
            out_specs=body,
            scratch_shapes=[
                pltpu.VMEM((2, rows + 2, width + 2 * MARGIN, LANES), jnp.float32)
            ],
        ),
        out_shape=jax.ShapeDtypeStruct(shape, jnp.bfloat16),
        input_output_aliases=aliases,
        compiler_params=pltpu.CompilerParams(
            dimension_semantics=("arbitrary",), vmem_limit_bytes=MIX_LIMIT
        ),
        cost_estimate=pl.CostEstimate(
            flops=2 * tokens * plan.blocks * LANES * LANES * 2,
            bytes_accessed=8 * tokens * plan.blocks * LANES,
            transcendentals=tokens * plan.blocks * LANES,
        ),
        name="mix",
    )(half, odd, *operands)


def swap(array, axis, bit):
    n = lax.axis_size(axis)
    return lax.ppermute(array, axis, [(i, i ^ bit) for i in range(n)])


def cross(edge):
    n_row, n_frame = lax.axis_size("row"), lax.axis_size("frame")
    pairs = [(i, i + 1) for i in range(1, n_row - 1, 2)]
    pairs = pairs + [(j, i) for i, j in pairs]
    if n_row != 4 or n_frame % 2:
        return lax.ppermute(edge, "row", pairs), lambda held: held
    both = ("frame", "row")
    one, two = [], []
    for f in range(n_frame):
        for i, j in pairs:
            corner = i ^ 2
            if f % 2:
                one.append((f * n_row + i, f * n_row + corner))
                two.append((f * n_row + corner, f * n_row + j))
            else:
                one.append((f * n_row + i, f * n_row + j))
                two.append((f * n_row + j, f * n_row + j))
    return lax.ppermute(edge, both, one), lambda held: lax.ppermute(held, both, two)


def per_device(queries, keys, values, gate, conv_weight):
    frames, rows, width, channels = queries.shape
    tokens = rows * width
    n_row, n_frame = lax.axis_size("row"), lax.axis_size("frame")
    me_row, me_frame = lax.axis_index("row"), lax.axis_index("frame")
    f32, bf16 = jnp.float32, jnp.bfloat16

    top = n_row // 2
    plan = Plan(channels, 2)
    own = (me_row // top).astype(jnp.int32).reshape(1)
    other = 1 - own

    keys = keys.reshape(frames, tokens, channels)
    values = values.reshape(frames, tokens, channels)
    odd = (me_row % 2).astype(jnp.int32).reshape(1)
    send, mine, far, *near = sums(plan, own, odd, keys, values, queries)
    got = swap(send, "row", top)
    far, forward = cross(far)
    near = [swap(edge, "row", 1) for edge in near]
    mine = mine + got.astype(f32)

    total = jnp.sum(mine, axis=0)
    moving = total.astype(bf16)
    neighbour = swap(moving, "frame", 1).astype(f32)
    second = (me_frame % 2) == 1
    before = jnp.where(second, neighbour, 0.0)
    running = total + neighbour
    pairs = n_frame // 2
    reach = 1
    while reach < pairs:
        hop = [(i, i + 2 * reach) for i in range(n_frame - 2 * reach)]
        moving = running.astype(bf16)
        if reach == 2:
            moving, far = lax.optimization_barrier((moving, far))
        earlier = lax.ppermute(moving, "frame", hop).astype(f32)
        before = before + earlier
        running = running + earlier
        reach *= 2
    states = before[None] + jnp.cumsum(mine, axis=0)
    bit = 1
    while bit < top:
        moving = states.astype(bf16)
        if bit == 1:
            moving, near[-1] = lax.optimization_barrier((moving, near[-1]))
            moving, queries, gate = lax.optimization_barrier((moving, queries, gate))
            qf, sg = ready(plan, queries, gate)
        arrived = swap(moving, "row", bit)
        if bit == 1:
            arrived, qf, sg = lax.optimization_barrier((arrived, qf, sg))
        states = states + arrived.astype(f32)
        bit *= 2
    states = states.astype(bf16)
    others = swap(states, "row", top)

    far = forward(far)
    shape = queries.shape
    out = mix(plan, shape, own, odd, states, qf, near, far, sg, conv_weight, None)
    return mix(plan, shape, other, odd, others, qf, near, far, sg, conv_weight, out)


def solution(mesh):
    spec = P("frame", "row", None, None)
    return jax.shard_map(
        per_device,
        mesh=mesh,
        in_specs=(spec, spec, spec, spec, P()),
        out_specs=spec,
        check_vma=False,
    )
```

time: 76.3 us -> 52.3 us (0.69)
  waiting for transfers between devices: 29 us -> 17.4 us
  local copies, waits for them, and re-layouts: 7.03 us -> 0.01 us
  starting transfers between devices: 21.6 us -> 18.4 us
  other arithmetic: 1.8 us -> 0.26 us
    ppermute x4 -> x5, waiting for transfers between devices: 27 us -> 16.1 us  [swap(): return lax.ppermute(array, axis, [(i, i ^ bit) for i in range(n)])]
    ppermute x4, starting transfers between devices: 16.3 us -> 9.6 us  [the longest x2 8.21 us: per_device(): earlier = lax.ppermute(moving, 'frame', hop).astype(f32)]
    pallas_call x2, Pallas kernels: 13.8 us -> 8.33 us  [mix(): pl.pallas_call(functools.partial(mix_kernel, plan, (frames, rows, width))...]
    pallas_call x2, Pallas kernels: 2.59 us -> 7.65 us  [the longest x1 4.46 us: ready(): pl.pallas_call(functools.partial(ready_kernel, plan), grid=(plan.halves *...]
    unnamed x14 -> x2, local copies, waits for them, and re-layouts: 5.01 us -> 0.01 us
    ppermute x4 -> x5, starting transfers between devices: 5.32 us -> 8.76 us  [swap(): return lax.ppermute(array, axis, [(i, i ^ bit) for i in range(n)])]
    slice x1 -> x0, local copies, waits for them, and re-layouts: 1.09 us -> none  [per_device(): down = lax.ppermute(queries[:, :1], 'row', [(j, i) for i, j in ring])]
    reshape x1 -> x0, local copies, waits for them, and re-layouts: 0.94 us -> none  [per_device(): weight = conv_weight.reshape(9, channels)]
  transfers between devices with their start and end apart: 8 -> 9, of which waited for: 4 -> 5; matrix products, arithmetic and copies ran while one was open for 4% -> 0% of each run, Pallas kernels for 11% -> 17%
where the time goes in v2:
time: 52.3 us; the launch traced here: 52.1 us
  starting transfers between devices  18.4 us (35%)
  waiting for transfers between devices  17.4 us (33%)
  Pallas kernels  16 us (31%)
    ppermute x5, waiting for transfers between devices, swap(): return lax.ppermute(array, axis, [(i, i ^ bit) for i in range(n)])  16.1 us
    ppermute x5, starting transfers between devices, swap(): return lax.ppermute(array, axis, [(i, i ^ bit) for i in range(n)])  8.76 us
    pallas_call x2, Pallas kernels, mix(): pl.pallas_call(functools.partial(mix_kernel, plan, (frames, rows, width))...  8.33 us
    ppermute x2, starting transfers between devices, per_device(): earlier = lax.ppermute(moving, 'frame', hop).astype(f32)  8.21 us
    pallas_call x1, Pallas kernels, ready(): pl.pallas_call(functools.partial(ready_kernel, plan), grid=(plan.halves *...  4.46 us
    pallas_call x1, Pallas kernels, sums(): pl.pallas_call(functools.partial(sums_kernel, plan), in_specs=[scalar, sc...  3.19 us
    ppermute x2, waiting for transfers between devices, per_device(): earlier = lax.ppermute(moving, 'frame', hop).astype(f32)  1.28 us
  transfers between devices with their start and end apart: 9, of which 5 were waited for; matrix products, arithmetic and copies ran while one was open for 0% of the time, Pallas kernels for 17%

profile of v2, /device:TPU:0, one launch (start us, length us, event | category | flops | bytes accessed | tf_op | source)
XLA Modules:
  0.0 52.1 jit_solution(9004337010980931647)
XLA Ops:
  0.0 3.2 %sums.1 = (bf16[2,304,128]{2,1,0:T(8,128)(2,1)S(1)}, f32[2,304,128]{2,1,0:T(8,128)S(1)}, bf16[2,1,64,2240]{3,2,1,0:T(8,128)(2,1)S(1)}, bf16[2,1,64,2240]{3,2,1,0:T(8,128)(2,1)S(1)}) custom-call(s32[1]{0:T(128)} %bitcast.own_ref.half_ref, s32[1]{0:T(128)} %bitcast.1.odd_ref, bf16[2,256,2240]{2,1,0:T(8,128)(2,1)} %bitcast.4, bf16[2,256,2240]{2,1,0:T(8,128)(2,1)} %bitcast.5, ...), custom_call_target="tpu_custom_call" | custom-call | flops 293601280 | bytes 4587520 | tf_op jit(solution)/shard_map/sums/pallas_call | solution.py:128
  3.2 3.0 %collective-permute-start = (bf16[2,304,128]{2,1,0:T(8,128)(2,1)S(1)}, bf16[2,304,128]{2,1,0:T(8,128)(2,1)S(1)}, u32[]{:S(2)}, u32[]{:S(2)}) collective-permute-start(bf16[2,304,128]{2,1,0:T(8,128)(2,1)S(1)} %get-tuple-element.22), channel_id=1, source_target_pairs={{0,2},{1,3},{2,0},{3,1},{4,6},{5,7},{6,4},{7,5},{8,10},{9,11},{10,... | collective-permute-start | bytes 466952 | tf_op jit(solution)/shard_map/ppermute | solution.py:314
  6.2 4.0 %collective-permute-done = bf16[2,304,128]{2,1,0:T(8,128)(2,1)S(1)} collective-permute-done((bf16[2,304,128]{2,1,0:T(8,128)(2,1)S(1)}, bf16[2,304,128]{2,1,0:T(8,128)(2,1)S(1)}, u32[]{:S(2)}, u32[]{:S(2)}) %collective-permute-start) | collective-permute-done | bytes 155680 | tf_op jit(solution)/shard_map/ppermute | solution.py:314
  10.3 0.1 collective-permute-start.1
  10.4 0.7 %collective-permute-start.3 = (bf16[2,1,64,2240]{3,2,1,0:T(8,128)(2,1)S(1)}, bf16[2,1,64,2240]{3,2,1,0:T(8,128)(2,1)S(1)}, u32[]{:S(2)}, u32[]{:S(2)}) collective-permute-start(bf16[2,1,64,2240]{3,2,1,0:T(8,128)(2,1)S(1)} %get-tuple-element.23), channel_id=1, source_target_pairs={{1,2},{2,1},{5,7},{6,4},{9,10},{10,9},{13,15},{14,12},{17,18},{18,... | collective-permute-start | bytes 1720328 | tf_op jit(solution)/shard_map/ppermute | solution.py:334
  11.1 0.6 %collective-permute-done.1 = bf16[304,128]{1,0:T(8,128)(2,1)S(1)} collective-permute-done((bf16[304,128]{1,0:T(8,128)(2,1)S(1)}, bf16[304,128]{1,0:T(8,128)(2,1)S(1)}, u32[]{:S(2)}, u32[]{:S(2)}) %collective-permute-start.1) | collective-permute-done | bytes 77856 | tf_op jit(solution)/shard_map/ppermute | solution.py:314
  11.7 3.7 %collective-permute-start.2 = (bf16[304,128]{1,0:T(8,128)(2,1)S(1)}, bf16[304,128]{1,0:T(8,128)(2,1)S(1)}, u32[]{:S(2)}, u32[]{:S(2)}) collective-permute-start(bf16[304,128]{1,0:T(8,128)(2,1)S(1)} %fusion.4), channel_id=1, source_target_pairs={{0,8},{4,12},{8,16},{12,20},{16,24},{20,28},{1,9},{5,13},{9,17},{1... | collective-permute-start | bytes 233480 | tf_op jit(solution)/shard_map/ppermute | solution.py:371
  15.4 3.7 %collective-permute-start.5 = (bf16[2,1,64,2240]{3,2,1,0:T(8,128)(2,1)S(1)}, bf16[2,1,64,2240]{3,2,1,0:T(8,128)(2,1)S(1)}, u32[]{:S(2)}, u32[]{:S(2)}) collective-permute-start(bf16[2,1,64,2240]{3,2,1,0:T(8,128)(2,1)S(1)} %get-tuple-element.25), channel_id=1, source_target_pairs={{0,1},{1,0},{2,3},{3,2},{4,5},{5,4},{6,7},{7,6},{8,9},{9,8},{10,11... | collective-permute-start | bytes 1720328 | tf_op jit(solution)/shard_map/ppermute | solution.py:314
  19.1 0.0 collective-permute-done.2
  19.1 0.0 collective-permute-done.3
  19.2 4.5 %collective-permute-start.4 = (bf16[304,128]{1,0:T(8,128)(2,1)S(1)}, bf16[304,128]{1,0:T(8,128)(2,1)S(1)}, u32[]{:S(2)}, u32[]{:S(2)}) collective-permute-start(bf16[304,128]{1,0:T(8,128)(2,1)S(1)} %fusion.3), channel_id=1, source_target_pairs={{0,16},{4,20},{8,24},{12,28},{1,17},{5,21},{9,25},{13,29},{2,18},{... | collective-permute-start | bytes 233480 | tf_op jit(solution)/shard_map/ppermute | solution.py:371
  23.7 0.7 %collective-permute-start.8 = (bf16[2,1,64,2240]{3,2,1,0:T(8,128)(2,1)S(1)}, bf16[2,1,64,2240]{3,2,1,0:T(8,128)(2,1)S(1)}, u32[]{:S(2)}, u32[]{:S(2)}) collective-permute-start(bf16[2,1,64,2240]{3,2,1,0:T(8,128)(2,1)S(1)} %collective-permute-done.3), channel_id=1, source_target_pairs={{2,2},{1,1},{7,6},{4,5},{10,10},{9,9},{15,14},{12,13},{18,18},{17,... | collective-permute-start | bytes 1720328 | tf_op jit(solution)/shard_map/ppermute | solution.py:334
  24.4 1.3 %collective-permute-done.4 = bf16[304,128]{1,0:T(8,128)(2,1)S(1)} collective-permute-done((bf16[304,128]{1,0:T(8,128)(2,1)S(1)}, bf16[304,128]{1,0:T(8,128)(2,1)S(1)}, u32[]{:S(2)}, u32[]{:S(2)}) %collective-permute-start.4) | collective-permute-done | bytes 77856 | tf_op jit(solution)/shard_map/ppermute | solution.py:371
  25.7 0.1 add_convert_fusion.1
  25.8 10.7 %collective-permute-done.5.rest_0_ = bf16[2,1,64,2240]{3,2,1,0:T(8,128)(2,1)S(1)} collective-permute-done((bf16[2,1,64,2240]{3,2,1,0:T(8,128)(2,1)S(1)}, bf16[2,1,64,2240]{3,2,1,0:T(8,128)(2,1)S(1)}, u32[]{:S(2)}, u32[]{:S(2)}) %collective-permute-start.5) | collective-permute-done | bytes 573472 | tf_op jit(solution)/shard_map/ppermute | solution.py:314
  36.5 0.0 copy-start
  36.5 0.0 collective-permute-start.6
  36.5 4.5 %ready.1 = (bf16[18,2,256,128]{3,2,1,0:T(8,128)(2,1)S(1)}, f32[18,2,256,128]{3,2,1,0:T(8,128)S(1)}) custom-call(bf16[2,4,64,2240]{3,2,1,0:T(8,128)(2,1)} %q_ref, bf16[2,4,64,2240]{3,2,1,0:T(8,128)(2,1)} %g_ref), custom_call_target="tpu_custom_call" | custom-call | flops 9175040 | bytes 11468800 | tf_op jit(solution)/shard_map/ready/pallas_call | solution.py:174
  41.0 0.8 %collective-permute-done.6 = bf16[2,304,128]{2,1,0:T(8,128)(2,1)S(1)} collective-permute-done((bf16[2,304,128]{2,1,0:T(8,128)(2,1)S(1)}, bf16[2,304,128]{2,1,0:T(8,128)(2,1)S(1)}, u32[]{:S(2)}, u32[]{:S(2)}) %collective-permute-start.6) | collective-permute-done | bytes 155680 | tf_op jit(solution)/shard_map/ppermute | solution.py:314
  41.7 0.1 add_convert_fusion.s_ref
  41.8 1.9 %collective-permute-start.7 = (bf16[2,304,128]{2,1,0:T(8,128)(2,1)S(1)}, bf16[2,304,128]{2,1,0:T(8,128)(2,1)S(1)}, u32[]{:S(2)}, u32[]{:S(2)}) collective-permute-start(bf16[2,304,128]{2,1,0:T(8,128)(2,1)S(1)} %add_convert_fusion.s_ref), channel_id=1, source_target_pairs={{0,2},{1,3},{2,0},{3,1},{4,6},{5,7},{6,4},{7,5},{8,10},{9,11},{10,... | collective-permute-start | bytes 466952 | tf_op jit(solution)/shard_map/ppermute | solution.py:314
  43.7 0.0 collective-permute-done.8.far_ref
  43.8 0.0 copy-done
  43.8 4.2 %mix.2.rest_1_ = bf16[2,4,64,2240]{3,2,1,0:T(8,128)(2,1)} custom-call(s32[1]{0:T(128)} %bitcast.own_ref.half_ref, s32[1]{0:T(128)} %bitcast.1.odd_ref, bf16[2,304,128]{2,1,0:T(8,128)(2,1)S(1)} %add_convert_fusion.s_ref, bf16[18,2,256,128]{3,2,1,0:T(8,128)(2,1)S(1)} %get-tuple-element.33.qf_ref, f32[18,2,256,128]{3,2,1,0:T(8,128)S(1)} %get-tuple-element.34.sg_ref, ...), custom_call_target="tpu_custom_call" | custom-call | flops 452984832 | bytes 7077888 | tf_op jit(solution)/shard_map/mix/pallas_call | solution.py:287
  47.9 0.0 collective-permute-done.7.s_ref
  47.9 4.2 %mix.3 = bf16[2,4,64,2240]{3,2,1,0:T(8,128)(2,1)} custom-call(s32[1]{0:T(128)S(6)} %sub.8.half_ref, s32[1]{0:T(128)} %bitcast.1.odd_ref, bf16[2,304,128]{2,1,0:T(8,128)(2,1)S(1)} %collective-permute-done.7.s_ref, bf16[18,2,256,128]{3,2,1,0:T(8,128)(2,1)S(1)} %get-tuple-element.33.qf_ref, ...), custom_call_target="tpu_custom_call", output_to_operand_aliasing={{}: (8, {})} | custom-call | flops 452984832 | bytes 7077888 | tf_op jit(solution)/shard_map/mix/pallas_call | solution.py:287
  (5 shorter events, 0.1 us)
Async XLA Ops:
  3.2 7.1 %collective-permute-start = (bf16[2,304,128]{2,1,0:T(8,128)(2,1)S(1)}, bf16[2,304,128]{2,1,0:T(8,128)(2,1)S(1)}, u32[]{:S(2)}, u32[]{:S(2)}) collective-permute-start(bf16[2,304,128]{2,1,0:T(8,128)(2,1)S(1)} %get-tuple-element.22), channel_id=1, source_target_pairs={{0,2},{1,3},{2,0},{3,1},{4,6},{5,7},{6,4},{7,5},{8,10},{9,11},{10,... | collective-permute-start | bytes 466952 | tf_op jit(solution)/shard_map/ppermute | solution.py:314
  10.3 1.3 %collective-permute-start.1 = (bf16[304,128]{1,0:T(8,128)(2,1)S(1)}, bf16[304,128]{1,0:T(8,128)(2,1)S(1)}, u32[]{:S(2)}, u32[]{:S(2)}) collective-permute-start(bf16[304,128]{1,0:T(8,128)(2,1)S(1)} %convert_element_type.31), channel_id=1, source_target_pairs={{0,4},{4,0},{8,12},{12,8},{16,20},{20,16},{24,28},{28,24},{1,5},{5... | collective-permute-start | bytes 233480 | tf_op jit(solution)/shard_map/ppermute | solution.py:314
  10.4 8.8 %collective-permute-start.3 = (bf16[2,1,64,2240]{3,2,1,0:T(8,128)(2,1)S(1)}, bf16[2,1,64,2240]{3,2,1,0:T(8,128)(2,1)S(1)}, u32[]{:S(2)}, u32[]{:S(2)}) collective-permute-start(bf16[2,1,64,2240]{3,2,1,0:T(8,128)(2,1)S(1)} %get-tuple-element.23), channel_id=1, source_target_pairs={{1,2},{2,1},{5,7},{6,4},{9,10},{10,9},{13,15},{14,12},{17,18},{18,... | collective-permute-start | bytes 1720328 | tf_op jit(solution)/shard_map/ppermute | solution.py:334
  11.7 7.4 %collective-permute-start.2 = (bf16[304,128]{1,0:T(8,128)(2,1)S(1)}, bf16[304,128]{1,0:T(8,128)(2,1)S(1)}, u32[]{:S(2)}, u32[]{:S(2)}) collective-permute-start(bf16[304,128]{1,0:T(8,128)(2,1)S(1)} %fusion.4), channel_id=1, source_target_pairs={{0,8},{4,12},{8,16},{12,20},{16,24},{20,28},{1,9},{5,13},{9,17},{1... | collective-permute-start | bytes 233480 | tf_op jit(solution)/shard_map/ppermute | solution.py:371
  15.4 21.1 %collective-permute-start.5 = (bf16[2,1,64,2240]{3,2,1,0:T(8,128)(2,1)S(1)}, bf16[2,1,64,2240]{3,2,1,0:T(8,128)(2,1)S(1)}, u32[]{:S(2)}, u32[]{:S(2)}) collective-permute-start(bf16[2,1,64,2240]{3,2,1,0:T(8,128)(2,1)S(1)} %get-tuple-element.25), channel_id=1, source_target_pairs={{0,1},{1,0},{2,3},{3,2},{4,5},{5,4},{6,7},{7,6},{8,9},{9,8},{10,11... | collective-permute-start | bytes 1720328 | tf_op jit(solution)/shard_map/ppermute | solution.py:314
  19.2 6.5 %collective-permute-start.4 = (bf16[304,128]{1,0:T(8,128)(2,1)S(1)}, bf16[304,128]{1,0:T(8,128)(2,1)S(1)}, u32[]{:S(2)}, u32[]{:S(2)}) collective-permute-start(bf16[304,128]{1,0:T(8,128)(2,1)S(1)} %fusion.3), channel_id=1, source_target_pairs={{0,16},{4,20},{8,24},{12,28},{1,17},{5,21},{9,25},{13,29},{2,18},{... | collective-permute-start | bytes 233480 | tf_op jit(solution)/shard_map/ppermute | solution.py:371
  23.7 20.1 %collective-permute-start.8 = (bf16[2,1,64,2240]{3,2,1,0:T(8,128)(2,1)S(1)}, bf16[2,1,64,2240]{3,2,1,0:T(8,128)(2,1)S(1)}, u32[]{:S(2)}, u32[]{:S(2)}) collective-permute-start(bf16[2,1,64,2240]{3,2,1,0:T(8,128)(2,1)S(1)} %collective-permute-done.3), channel_id=1, source_target_pairs={{2,2},{1,1},{7,6},{4,5},{10,10},{9,9},{15,14},{12,13},{18,18},{17,... | collective-permute-start | bytes 1720328 | tf_op jit(solution)/shard_map/ppermute | solution.py:334
  36.5 7.2 %copy-start = (f32[3,3,2240]{2,1,0:T(4,128)S(1)}, f32[3,3,2240]{2,1,0:T(4,128)}, u32[]{:S(2)}) copy-start(f32[3,3,2240]{2,1,0:T(4,128)} %w_ref.3) | copy-start | bytes 241924
  36.5 5.2 %collective-permute-start.6 = (bf16[2,304,128]{2,1,0:T(8,128)(2,1)S(1)}, bf16[2,304,128]{2,1,0:T(8,128)(2,1)S(1)}, u32[]{:S(2)}, u32[]{:S(2)}) collective-permute-start(bf16[2,304,128]{2,1,0:T(8,128)(2,1)S(1)} %get-tuple-element.27), channel_id=1, source_target_pairs={{0,1},{1,0},{2,3},{3,2},{4,5},{5,4},{6,7},{7,6},{8,9},{9,8},{10,11... | collective-permute-start | bytes 466952 | tf_op jit(solution)/shard_map/ppermute | solution.py:314
  41.8 6.1 %collective-permute-start.7 = (bf16[2,304,128]{2,1,0:T(8,128)(2,1)S(1)}, bf16[2,304,128]{2,1,0:T(8,128)(2,1)S(1)}, u32[]{:S(2)}, u32[]{:S(2)}) collective-permute-start(bf16[2,304,128]{2,1,0:T(8,128)(2,1)S(1)} %add_convert_fusion.s_ref), channel_id=1, source_target_pairs={{0,2},{1,3},{2,0},{3,1},{4,6},{5,7},{6,4},{7,5},{8,10},{9,11},{10,... | collective-permute-start | bytes 466952 | tf_op jit(solution)/shard_map/ppermute | solution.py:314

commit v3 on v2

--- a/solution.py
+++ b/solution.py
@@ -355,23 +355,35 @@
     near = [swap(edge, "row", 1) for edge in near]
     mine = mine + got.astype(f32)
 
+    second = (me_frame % 2) == 1
+    reaches = [1 << i for i in range((n_frame // 2 - 1).bit_length())]
+    once = jnp.minimum(me_frame + 1, 1)
+
+    def arriving(running, reach):
+        hop = [(i, i + 2 * reach) for i in range(n_frame - 2 * reach)]
+        return lax.ppermute(running.astype(bf16), "frame", hop).astype(f32)
+
+    def nearest(_, carry):
+        _, total = carry
+        neighbour = swap(total.astype(bf16), "frame", 1).astype(f32)
+        before, running = jnp.where(second, neighbour, 0.0), total + neighbour
+        for reach in reaches[:1]:
+            earlier = arriving(running, reach)
+            before, running = before + earlier, running + earlier
+        return before, running
+
+    def farther(_, before):
+        ahead = running
+        for reach in reaches[1:]:
+            earlier = arriving(ahead, reach)
+            before, ahead = before + earlier, ahead + earlier
+        return before
+
     total = jnp.sum(mine, axis=0)
-    moving = total.astype(bf16)
-    neighbour = swap(moving, "frame", 1).astype(f32)
-    second = (me_frame % 2) == 1
-    before = jnp.where(second, neighbour, 0.0)
-    running = total + neighbour
-    pairs = n_frame // 2
-    reach = 1
-    while reach < pairs:
-        hop = [(i, i + 2 * reach) for i in range(n_frame - 2 * reach)]
-        moving = running.astype(bf16)
-        if reach == 2:
-            moving, far = lax.optimization_barrier((moving, far))
-        earlier = lax.ppermute(moving, "frame", hop).astype(f32)
-        before = before + earlier
-        running = running + earlier
-        reach *= 2
+    before, running = lax.fori_loop(0, once, nearest, (total, total))
+    running, far = lax.optimization_barrier((running, far))
+    far = forward(far)
+    before = farther(0, before)
     states = before[None] + jnp.cumsum(mine, axis=0)
     bit = 1
     while bit < top:
@@ -388,7 +400,6 @@
     states = states.astype(bf16)
     others = swap(states, "row", top)
 
-    far = forward(far)
     shape = queries.shape
     out = mix(plan, shape, own, odd, states, qf, near, far, sg, conv_weight, None)
     return mix(plan, shape, other, odd, others, qf, near, far, sg, conv_weight, out)

time: 52.3 us -> 47.9 us (0.916)
  waiting for transfers between devices: 17.4 us -> 7.32 us
  starting transfers between devices: 18.4 us -> 21.7 us
  other arithmetic: 0.26 us -> 1.87 us
  local copies, waits for them, and re-layouts: 0.01 us -> 0.65 us
    ppermute x5, waiting for transfers between devices: 16.1 us -> 4.02 us  [swap(): return lax.ppermute(array, axis, [(i, i ^ bit) for i in range(n)])]
    ppermute x5, starting transfers between devices: 8.76 us -> 11.2 us  [swap(): return lax.ppermute(array, axis, [(i, i ^ bit) for i in range(n)])]
    ppermute x2, waiting for transfers between devices: 1.28 us -> 3.29 us  [arriving(): return lax.ppermute(running.astype(bf16), 'frame', hop).astype(f32)]
    add x1 -> x2, other arithmetic: 0.04 us -> 1.67 us  [the longest x1 0.93 us: farther(): before, ahead = (before + earlier, ahead + earlier)]
    ppermute x2, starting transfers between devices: 8.21 us -> 9.17 us  [arriving(): return lax.ppermute(running.astype(bf16), 'frame', hop).astype(f32)]
    unnamed x2 -> x5, local copies, waits for them, and re-layouts: 0.01 us -> 0.65 us
  transfers between devices with their start and end apart: 9 -> 9, of which waited for: 5 -> 7; matrix products, arithmetic and copies ran while one was open for 0% -> 4% of each run, Pallas kernels for 17% -> 18%
where the time goes in v3:
time: 47.9 us; the launch traced here: 47.6 us
  starting transfers between devices  21.7 us (45%)
  Pallas kernels  15.9 us (33%)
  waiting for transfers between devices  7.32 us (15%)
  other arithmetic  1.87 us (4%)
  local copies, waits for them, and re-layouts  0.65 us (1%)
    ppermute x5, starting transfers between devices, swap(): return lax.ppermute(array, axis, [(i, i ^ bit) for i in range(n)])  11.2 us
    ppermute x2, starting transfers between devices, arriving(): return lax.ppermute(running.astype(bf16), 'frame', hop).astype(f32)  9.17 us
    pallas_call x2, Pallas kernels, mix(): pl.pallas_call(functools.partial(mix_kernel, plan, (frames, rows, width))...  8.33 us
    pallas_call x1, Pallas kernels, ready(): pl.pallas_call(functools.partial(ready_kernel, plan), grid=(plan.halves *...  4.42 us
    ppermute x5, waiting for transfers between devices, swap(): return lax.ppermute(array, axis, [(i, i ^ bit) for i in range(n)])  4.02 us
    ppermute x2, waiting for transfers between devices, arriving(): return lax.ppermute(running.astype(bf16), 'frame', hop).astype(f32)  3.29 us
    pallas_call x1, Pallas kernels, sums(): pl.pallas_call(functools.partial(sums_kernel, plan), in_specs=[scalar, sc...  3.19 us
  transfers between devices with their start and end apart: 9, of which 7 were waited for; matrix products, arithmetic and copies ran while one was open for 4% of the time, Pallas kernels for 18%

profile of v3, /device:TPU:0, one launch (start us, length us, event | category | flops | bytes accessed | tf_op | source)
XLA Modules:
  0.0 47.6 jit_solution(8260403678980294603)
XLA Ops:
  0.0 3.2 %sums.1 = (bf16[2,304,128]{2,1,0:T(8,128)(2,1)S(1)}, f32[2,304,128]{2,1,0:T(8,128)S(1)}, bf16[2,1,64,2240]{3,2,1,0:T(8,128)(2,1)S(1)}, bf16[2,1,64,2240]{3,2,1,0:T(8,128)(2,1)S(1)}) custom-call(s32[1]{0:T(128)} %bitcast.own_ref.half_ref, s32[1]{0:T(128)} %bitcast.1.odd_ref, bf16[2,256,2240]{2,1,0:T(8,128)(2,1)} %bitcast.4, bf16[2,256,2240]{2,1,0:T(8,128)(2,1)} %bitcast.5, ...), custom_call_target="tpu_custom_call" | custom-call | flops 293601280 | bytes 4587520 | tf_op jit(solution)/shard_map/sums/pallas_call | solution.py:128
  3.2 3.0 %collective-permute-start.2 = (bf16[2,304,128]{2,1,0:T(8,128)(2,1)S(1)}, bf16[2,304,128]{2,1,0:T(8,128)(2,1)S(1)}, u32[]{:S(2)}, u32[]{:S(2)}) collective-permute-start(bf16[2,304,128]{2,1,0:T(8,128)(2,1)S(1)} %get-tuple-element.50), channel_id=1, source_target_pairs={{0,2},{1,3},{2,0},{3,1},{4,6},{5,7},{6,4},{7,5},{8,10},{9,11},{10,... | collective-permute-start | bytes 466952 | tf_op jit(solution)/shard_map/ppermute | solution.py:314
  6.2 0.7 %collective-permute-start.3 = (bf16[2,1,64,2240]{3,2,1,0:T(8,128)(2,1)S(1)}, bf16[2,1,64,2240]{3,2,1,0:T(8,128)(2,1)S(1)}, u32[]{:S(2)}, u32[]{:S(2)}) collective-permute-start(bf16[2,1,64,2240]{3,2,1,0:T(8,128)(2,1)S(1)} %get-tuple-element.53), channel_id=1, source_target_pairs={{1,2},{2,1},{5,7},{6,4},{9,10},{10,9},{13,15},{14,12},{17,18},{18,... | collective-permute-start | bytes 1720328 | tf_op jit(solution)/shard_map/ppermute | solution.py:334
  6.9 2.8 %collective-permute-start.5 = (bf16[2,1,64,2240]{3,2,1,0:T(8,128)(2,1)S(1)}, bf16[2,1,64,2240]{3,2,1,0:T(8,128)(2,1)S(1)}, u32[]{:S(2)}, u32[]{:S(2)}) collective-permute-start(bf16[2,1,64,2240]{3,2,1,0:T(8,128)(2,1)S(1)} %get-tuple-element.55), channel_id=1, source_target_pairs={{0,1},{1,0},{2,3},{3,2},{4,5},{5,4},{6,7},{7,6},{8,9},{9,8},{10,11... | collective-permute-start | bytes 1720328 | tf_op jit(solution)/shard_map/ppermute | solution.py:314
  9.7 0.5 %collective-permute-done.2 = bf16[2,304,128]{2,1,0:T(8,128)(2,1)S(1)} collective-permute-done((bf16[2,304,128]{2,1,0:T(8,128)(2,1)S(1)}, bf16[2,304,128]{2,1,0:T(8,128)(2,1)S(1)}, u32[]{:S(2)}, u32[]{:S(2)}) %collective-permute-start.2) | collective-permute-done | bytes 155680 | tf_op jit(solution)/shard_map/ppermute | solution.py:314
  10.3 0.0 copy-start.1
  10.3 0.6 %copy-done.1 = f32[304,128]{1,0:T(8,128)} copy-done((f32[304,128]{1,0:T(8,128)}, f32[304,128]{1,0:T(8,128)S(1)}, u32[]{:S(2)}) %copy-start.1) | copy-done | bytes 155672
  11.0 8.0 %while.12 = (s32[]{:T(128)}, f32[304,128]{1,0:T(8,128)}, f32[304,128]{1,0:T(8,128)S(1)}, s32[]{:T(128)}, pred[]{:T(512)}, /*index=5*/s32[]{:T(128)}) while((s32[]{:T(128)}, f32[304,128]{1,0:T(8,128)}, f32[304,128]{1,0:T(8,128)S(1)}, s32[]{:T(128)}, pred[]{:T(512)}, /*index=5*/s32[]{:T(128)}) %tuple.33), condition=%wide.region_2.3_spmd, body=%wide.region_1.2_spmd.sunk | while | flops 389122 | bytes 1790102 | solution.py:383
  11.0 0.1 collective-permute-start
  11.1 1.3 %collective-permute-done = bf16[304,128]{1,0:T(8,128)(2,1)S(1)} collective-permute-done((bf16[304,128]{1,0:T(8,128)(2,1)S(1)}, bf16[304,128]{1,0:T(8,128)(2,1)S(1)}, u32[]{:S(2)}, u32[]{:S(2)}) %collective-permute-start) | collective-permute-done | bytes 77856 | tf_op jit(solution)/shard_map/while/body/ppermute | solution.py:314
  12.3 3.9 %collective-permute-start.1 = (bf16[304,128]{1,0:T(8,128)(2,1)S(1)}, bf16[304,128]{1,0:T(8,128)(2,1)S(1)}, u32[]{:S(2)}, u32[]{:S(2)}) collective-permute-start(bf16[304,128]{1,0:T(8,128)(2,1)S(1)} %fusion.4), channel_id=1, source_target_pairs={{0,8},{4,12},{8,16},{12,20},{16,24},{20,28},{1,9},{5,13},{9,17},{1... | collective-permute-start | bytes 233480 | tf_op jit(solution)/shard_map/while/body/ppermute | solution.py:364
  16.2 2.0 %collective-permute-done.1 = bf16[304,128]{1,0:T(8,128)(2,1)S(1)} collective-permute-done((bf16[304,128]{1,0:T(8,128)(2,1)S(1)}, bf16[304,128]{1,0:T(8,128)(2,1)S(1)}, u32[]{:S(2)}, u32[]{:S(2)}) %collective-permute-start.1) | collective-permute-done | bytes 77856 | tf_op jit(solution)/shard_map/while/body/ppermute | solution.py:364
  18.2 0.7 %convert_add_fusion.7 = (f32[304,128]{1,0:T(8,128)S(1)}, f32[304,128]{1,0:T(8,128)}) fusion(bf16[304,128]{1,0:T(8,128)(2,1)S(1)} %collective-permute-done.1, f32[304,128]{1,0:T(8,128)S(1)} %get-tuple-element.123, bf16[304,128]{1,0:T(8,128)(2,1)S(1)} %collective-permute-done, pred[]{:T(512)} %get-tuple-element.131), kind=kLoop, calls=%fused_computation.clone.1 | loop fusion | flops 233472 | bytes 622593 | tf_op jit(solution)/shard_map/while/body/add | solution.py:372
  18.9 0.0 collective-permute-done.3
  19.0 5.3 %collective-permute-start.4 = (bf16[304,128]{1,0:T(8,128)(2,1)S(1)}, bf16[304,128]{1,0:T(8,128)(2,1)S(1)}, u32[]{:S(2)}, u32[]{:S(2)}) collective-permute-start(bf16[304,128]{1,0:T(8,128)(2,1)S(1)} %convert_element_type.31), channel_id=1, source_target_pairs={{0,16},{4,20},{8,24},{12,28},{1,17},{5,21},{9,25},{13,29},{2,18},{... | collective-permute-start | bytes 233480 | tf_op jit(solution)/shard_map/ppermute | solution.py:364
  24.3 0.7 %collective-permute-start.8 = (bf16[2,1,64,2240]{3,2,1,0:T(8,128)(2,1)S(1)}, bf16[2,1,64,2240]{3,2,1,0:T(8,128)(2,1)S(1)}, u32[]{:S(2)}, u32[]{:S(2)}) collective-permute-start(bf16[2,1,64,2240]{3,2,1,0:T(8,128)(2,1)S(1)} %collective-permute-done.3), channel_id=1, source_target_pairs={{2,2},{1,1},{7,6},{4,5},{10,10},{9,9},{15,14},{12,13},{18,18},{17,... | collective-permute-start | bytes 1720328 | tf_op jit(solution)/shard_map/ppermute | solution.py:334
  25.0 1.3 %collective-permute-done.4 = bf16[304,128]{1,0:T(8,128)(2,1)S(1)} collective-permute-done((bf16[304,128]{1,0:T(8,128)(2,1)S(1)}, bf16[304,128]{1,0:T(8,128)(2,1)S(1)}, u32[]{:S(2)}, u32[]{:S(2)}) %collective-permute-start.4) | collective-permute-done | bytes 77856 | tf_op jit(solution)/shard_map/ppermute | solution.py:364
  26.3 0.9 %convert_add_fusion.5 = f32[304,128]{1,0:T(8,128)S(1)} fusion(f32[304,128]{1,0:T(8,128)} %get-tuple-element.51, bf16[304,128]{1,0:T(8,128)(2,1)S(1)} %collective-permute-done.4), kind=kLoop, calls=%fused_computation.10 | loop fusion | flops 77824 | bytes 389120 | tf_op jit(solution)/shard_map/add | solution.py:379
  27.2 0.1 add_convert_fusion.1
  27.3 2.1 %collective-permute-done.5.rest_0_ = bf16[2,1,64,2240]{3,2,1,0:T(8,128)(2,1)S(1)} collective-permute-done((bf16[2,1,64,2240]{3,2,1,0:T(8,128)(2,1)S(1)}, bf16[2,1,64,2240]{3,2,1,0:T(8,128)(2,1)S(1)}, u32[]{:S(2)}, u32[]{:S(2)}) %collective-permute-start.5) | collective-permute-done | bytes 573472 | tf_op jit(solution)/shard_map/ppermute | solution.py:314
  29.3 0.0 copy-start
  29.3 2.8 %collective-permute-start.6 = (bf16[2,304,128]{2,1,0:T(8,128)(2,1)S(1)}, bf16[2,304,128]{2,1,0:T(8,128)(2,1)S(1)}, u32[]{:S(2)}, u32[]{:S(2)}) collective-permute-start(bf16[2,304,128]{2,1,0:T(8,128)(2,1)S(1)} %get-tuple-element.57), channel_id=1, source_target_pairs={{0,1},{1,0},{2,3},{3,2},{4,5},{5,4},{6,7},{7,6},{8,9},{9,8},{10,11... | collective-permute-start | bytes 466952 | tf_op jit(solution)/shard_map/ppermute | solution.py:314
  32.1 4.4 %ready.1 = (bf16[18,2,256,128]{3,2,1,0:T(8,128)(2,1)S(1)}, f32[18,2,256,128]{3,2,1,0:T(8,128)S(1)}) custom-call(bf16[2,4,64,2240]{3,2,1,0:T(8,128)(2,1)} %q_ref, bf16[2,4,64,2240]{3,2,1,0:T(8,128)(2,1)} %g_ref), custom_call_target="tpu_custom_call" | custom-call | flops 9175040 | bytes 11468800 | tf_op jit(solution)/shard_map/ready/pallas_call | solution.py:174
  36.5 0.1 collective-permute-done.6
  36.6 0.1 add_convert_fusion.s_ref
  36.6 2.5 %collective-permute-start.7 = (bf16[2,304,128]{2,1,0:T(8,128)(2,1)S(1)}, bf16[2,304,128]{2,1,0:T(8,128)(2,1)S(1)}, u32[]{:S(2)}, u32[]{:S(2)}) collective-permute-start(bf16[2,304,128]{2,1,0:T(8,128)(2,1)S(1)} %add_convert_fusion.s_ref), channel_id=1, source_target_pairs={{0,2},{1,3},{2,0},{3,1},{4,6},{5,7},{6,4},{7,5},{8,10},{9,11},{10,... | collective-permute-start | bytes 466952 | tf_op jit(solution)/shard_map/ppermute | solution.py:314
  39.2 0.0 collective-permute-done.8.far_ref
  39.2 0.0 copy-done
  39.2 4.2 %mix.2.rest_1_ = bf16[2,4,64,2240]{3,2,1,0:T(8,128)(2,1)} custom-call(s32[1]{0:T(128)} %bitcast.own_ref.half_ref, s32[1]{0:T(128)} %bitcast.1.odd_ref, bf16[2,304,128]{2,1,0:T(8,128)(2,1)S(1)} %add_convert_fusion.s_ref, bf16[18,2,256,128]{3,2,1,0:T(8,128)(2,1)S(1)} %get-tuple-element.63.qf_ref, f32[18,2,256,128]{3,2,1,0:T(8,128)S(1)} %get-tuple-element.64.sg_ref, ...), custom_call_target="tpu_custom_call" | custom-call | flops 452984832 | bytes 7077888 | tf_op jit(solution)/shard_map/mix/pallas_call | solution.py:287
  43.4 0.1 collective-permute-done.7.s_ref
  43.5 4.2 %mix.3 = bf16[2,4,64,2240]{3,2,1,0:T(8,128)(2,1)} custom-call(s32[1]{0:T(128)S(6)} %sub.8.half_ref, s32[1]{0:T(128)} %bitcast.1.odd_ref, bf16[2,304,128]{2,1,0:T(8,128)(2,1)S(1)} %collective-permute-done.7.s_ref, bf16[18,2,256,128]{3,2,1,0:T(8,128)(2,1)S(1)} %get-tuple-element.63.qf_ref, ...), custom_call_target="tpu_custom_call", output_to_operand_aliasing={{}: (8, {})} | custom-call | flops 452984832 | bytes 7077888 | tf_op jit(solution)/shard_map/mix/pallas_call | solution.py:287
  (5 shorter events, 0.1 us)
Async XLA Ops:
  3.2 7.1 %collective-permute-start.2 = (bf16[2,304,128]{2,1,0:T(8,128)(2,1)S(1)}, bf16[2,304,128]{2,1,0:T(8,128)(2,1)S(1)}, u32[]{:S(2)}, u32[]{:S(2)}) collective-permute-start(bf16[2,304,128]{2,1,0:T(8,128)(2,1)S(1)} %get-tuple-element.50), channel_id=1, source_target_pairs={{0,2},{1,3},{2,0},{3,1},{4,6},{5,7},{6,4},{7,5},{8,10},{9,11},{10,... | collective-permute-start | bytes 466952 | tf_op jit(solution)/shard_map/ppermute | solution.py:314
  6.2 12.7 %collective-permute-start.3 = (bf16[2,1,64,2240]{3,2,1,0:T(8,128)(2,1)S(1)}, bf16[2,1,64,2240]{3,2,1,0:T(8,128)(2,1)S(1)}, u32[]{:S(2)}, u32[]{:S(2)}) collective-permute-start(bf16[2,1,64,2240]{3,2,1,0:T(8,128)(2,1)S(1)} %get-tuple-element.53), channel_id=1, source_target_pairs={{1,2},{2,1},{5,7},{6,4},{9,10},{10,9},{13,15},{14,12},{17,18},{18,... | collective-permute-start | bytes 1720328 | tf_op jit(solution)/shard_map/ppermute | solution.py:334
  6.9 22.4 %collective-permute-start.5 = (bf16[2,1,64,2240]{3,2,1,0:T(8,128)(2,1)S(1)}, bf16[2,1,64,2240]{3,2,1,0:T(8,128)(2,1)S(1)}, u32[]{:S(2)}, u32[]{:S(2)}) collective-permute-start(bf16[2,1,64,2240]{3,2,1,0:T(8,128)(2,1)S(1)} %get-tuple-element.55), channel_id=1, source_target_pairs={{0,1},{1,0},{2,3},{3,2},{4,5},{5,4},{6,7},{7,6},{8,9},{9,8},{10,11... | collective-permute-start | bytes 1720328 | tf_op jit(solution)/shard_map/ppermute | solution.py:314
  10.3 0.7 %copy-start.1 = (f32[304,128]{1,0:T(8,128)}, f32[304,128]{1,0:T(8,128)S(1)}, u32[]{:S(2)}) copy-start(f32[304,128]{1,0:T(8,128)S(1)} %fusion.2) | copy-start | bytes 466948
  11.0 1.3 %collective-permute-start = (bf16[304,128]{1,0:T(8,128)(2,1)S(1)}, bf16[304,128]{1,0:T(8,128)(2,1)S(1)}, u32[]{:S(2)}, u32[]{:S(2)}) collective-permute-start(bf16[304,128]{1,0:T(8,128)(2,1)S(1)} %convert_element_type.66), channel_id=1, source_target_pairs={{0,4},{4,0},{8,12},{12,8},{16,20},{20,16},{24,28},{28,24},{1,5},{5... | collective-permute-start | bytes 233480 | tf_op jit(solution)/shard_map/while/body/ppermute | solution.py:314
  12.3 5.9 %collective-permute-start.1 = (bf16[304,128]{1,0:T(8,128)(2,1)S(1)}, bf16[304,128]{1,0:T(8,128)(2,1)S(1)}, u32[]{:S(2)}, u32[]{:S(2)}) collective-permute-start(bf16[304,128]{1,0:T(8,128)(2,1)S(1)} %fusion.4), channel_id=1, source_target_pairs={{0,8},{4,12},{8,16},{12,20},{16,24},{20,28},{1,9},{5,13},{9,17},{1... | collective-permute-start | bytes 233480 | tf_op jit(solution)/shard_map/while/body/ppermute | solution.py:364
  19.0 7.3 %collective-permute-start.4 = (bf16[304,128]{1,0:T(8,128)(2,1)S(1)}, bf16[304,128]{1,0:T(8,128)(2,1)S(1)}, u32[]{:S(2)}, u32[]{:S(2)}) collective-permute-start(bf16[304,128]{1,0:T(8,128)(2,1)S(1)} %convert_element_type.31), channel_id=1, source_target_pairs={{0,16},{4,20},{8,24},{12,28},{1,17},{5,21},{9,25},{13,29},{2,18},{... | collective-permute-start | bytes 233480 | tf_op jit(solution)/shard_map/ppermute | solution.py:364
  24.3 14.9 %collective-permute-start.8 = (bf16[2,1,64,2240]{3,2,1,0:T(8,128)(2,1)S(1)}, bf16[2,1,64,2240]{3,2,1,0:T(8,128)(2,1)S(1)}, u32[]{:S(2)}, u32[]{:S(2)}) collective-permute-start(bf16[2,1,64,2240]{3,2,1,0:T(8,128)(2,1)S(1)} %collective-permute-done.3), channel_id=1, source_target_pairs={{2,2},{1,1},{7,6},{4,5},{10,10},{9,9},{15,14},{12,13},{18,18},{17,... | collective-permute-start | bytes 1720328 | tf_op jit(solution)/shard_map/ppermute | solution.py:334
  29.3 9.8 %copy-start = (f32[3,3,2240]{2,1,0:T(4,128)S(1)}, f32[3,3,2240]{2,1,0:T(4,128)}, u32[]{:S(2)}) copy-start(f32[3,3,2240]{2,1,0:T(4,128)} %w_ref.3) | copy-start | bytes 241924
  29.3 7.2 %collective-permute-start.6 = (bf16[2,304,128]{2,1,0:T(8,128)(2,1)S(1)}, bf16[2,304,128]{2,1,0:T(8,128)(2,1)S(1)}, u32[]{:S(2)}, u32[]{:S(2)}) collective-permute-start(bf16[2,304,128]{2,1,0:T(8,128)(2,1)S(1)} %get-tuple-element.57), channel_id=1, source_target_pairs={{0,1},{1,0},{2,3},{3,2},{4,5},{5,4},{6,7},{7,6},{8,9},{9,8},{10,11... | collective-permute-start | bytes 466952 | tf_op jit(solution)/shard_map/ppermute | solution.py:314
  36.6 6.8 %collective-permute-start.7 = (bf16[2,304,128]{2,1,0:T(8,128)(2,1)S(1)}, bf16[2,304,128]{2,1,0:T(8,128)(2,1)S(1)}, u32[]{:S(2)}, u32[]{:S(2)}) collective-permute-start(bf16[2,304,128]{2,1,0:T(8,128)(2,1)S(1)} %add_convert_fusion.s_ref), channel_id=1, source_target_pairs={{0,2},{1,3},{2,0},{3,1},{4,6},{5,7},{6,4},{7,5},{8,10},{9,11},{10,... | collective-permute-start | bytes 466952 | tf_op jit(solution)/shard_map/ppermute | solution.py:314
